TPU v7x, 32 devices: a whole 2x2x4 slice. The times are simulated.
32 devices in a mesh: ctx: 8 (over z, x), wa: 4 (over y, core).
Axes of the slice: x: 2, y: 2, z: 4, core: 2. Of those that a mesh axis runs over, the one named last changes fastest.
Arguments:
- tokens: bfloat16 [4, 1024, 1536], P('wa', 'ctx'), may hold values from -6 to 6
- teacher: float32 [4, 1024, 1536], P('wa', 'ctx'), may hold values from -6 to 6
- lengths: int32 [4], replicated, may hold values from 897 to 1024, as said below
- routes: int32 [4, 1024, 6], P('wa', 'ctx'), may hold values from 0 to 15, all different within a row; in each aligned block of 128 rows (0 to 127, 128 to 255, ..., all dimensions but the last counted through in order) at most 96 rows name the same one
- query_weight: bfloat16 [1536, 1536], P('wa'), may hold values from -0.15625 to 0.15625
- key_projection_matrix: bfloat16 [1536, 512], P('wa'), may hold values from -0.15625 to 0.15625
- value_projection_matrix: bfloat16 [1536, 512], P('wa'), may hold values from -0.15625 to 0.15625
- output_weight: bfloat16 [1536, 1536], P('wa'), may hold values from -0.4375 to 0.4375
- attn_gain: bfloat16 [1536], P('wa'), may hold values from 0.5 to 1.5
- moe_gain: bfloat16 [1536], P('wa'), may hold values from 0.5 to 1.5
- router_weight: bfloat16 [1536, 16], P('wa'), may hold values from -0.078125 to 0.078125
- shared_gate: bfloat16 [1536, 1024], P('wa'), may hold values from -0.15625 to 0.15625
- shared_up: bfloat16 [1536, 1024], P('wa'), may hold values from -0.15625 to 0.15625
- shared_down: bfloat16 [1536, 1024], P('wa'), may hold values from -0.1875 to 0.1875
- expert_gate: bfloat16 [16, 1536, 512], P('wa'), may hold values from -0.15625 to 0.15625
- expert_up: bfloat16 [16, 1536, 512], P('wa'), may hold values from -0.15625 to 0.15625
- expert_down: bfloat16 [16, 1536, 512], P('wa'), may hold values from -0.25 to 0.25
Outputs:
- block_out: bfloat16 [4, 1024, 1536], P('wa', 'ctx')
- grad_tokens: float32 [4, 1024, 1536], P('wa', 'ctx')
- grad_query: float32 [1536, 1536], P(('ctx', 'wa'))
- grad_key: float32 [1536, 512], P(('ctx', 'wa'))
- grad_value: float32 [1536, 512], P(('ctx', 'wa'))
- grad_output: float32 [1536, 1536], P(('ctx', 'wa'))
- grad_attn_gain: float32 [1536], P(('ctx', 'wa'))
- grad_moe_gain: float32 [1536], P(('ctx', 'wa'))
- grad_router: float32 [1536, 16], P(('ctx', 'wa'))
- grad_shared_gate: float32 [1536, 1024], P(('ctx', 'wa'))
- grad_shared_up: float32 [1536, 1024], P(('ctx', 'wa'))
- grad_shared_down: float32 [1536, 1024], P(('ctx', 'wa'))
- grad_expert_gate: float32 [16, 1536, 512], P('wa', 'ctx')
- grad_expert_up: float32 [16, 1536, 512], P('wa', 'ctx')
- grad_expert_down: float32 [16, 1536, 512], P('wa', 'ctx')
- loss: float32 [], replicated
Inputs may be any that keep to these rules, and one draw needn't show every extreme that they name: `lengths`: every sequence reaches into the last block of 128 positions; one is exactly 1024 long. `routes`: a position names 6 different experts; within the 128 positions of one device no expert is named more than 96 times, a bound that some block reaches.
All inputs are finite; a program needn't handle non-finite values.
Results may differ from a plain program's by a relative error of at most 0.029.
Values may be sent and summed in bfloat16 or wider, within the bound.
No kernel may reach another device: no remote copies, remote signals or barrier semaphores. Data moves between devices by JAX's collectives and lax.ppermute only.
A program may use at most 320 MiB of HBM per device.

v0:
```python
import jax
import jax.numpy as jnp
from jax import lax
from jax.sharding import PartitionSpec as P

QUERY_HEADS = 12
KEY_VALUE_HEADS = 4
HEAD_SIZE = 128
TOP = 6


epsilon = 1e-06
score_after_mask = -1e30
highest = lax.Precision.HIGHEST


def silu_parts(input_rows):
    sigma = jax.nn.sigmoid(input_rows)
    return (input_rows * sigma, sigma * (1.0 + input_rows * (1.0 - sigma)))


def inner_size(total):
    size_now = total
    while size_now > 512 and size_now % 2 == 0:
        size_now = size_now // 2
    return size_now


def norm_forward(value_rows, gain):
    factor = lax.rsqrt(jnp.mean(value_rows * value_rows, axis=-1, keepdims=True) + epsilon)
    return (value_rows * factor * gain, factor)


def norm_backward(value_rows, factor, gain, upstream):
    weighted = upstream * gain
    features = value_rows.shape[-1]
    inner_sum = jnp.sum(weighted * value_rows, axis=-1, keepdims=True)
    value_gradient_rows = (
        factor * weighted - value_rows * factor * factor * factor * inner_sum / features
    )
    grad_gain = jnp.sum(upstream * value_rows * factor, axis=0)
    return (value_gradient_rows, grad_gain)


def per_device(
    tokens,
    teacher,
    lengths,
    routes,
    query_weight,
    key_projection_matrix,
    value_projection_matrix,
    output_weight,
    attn_gain,
    moe_gain,
    router_weight,
    shared_gate,
    shared_up,
    shared_down,
    expert_gate,
    expert_up,
    expert_down,
):
    seq_index = lax.axis_index("wa")
    block_index = lax.axis_index("ctx")
    local_row_count = tokens.shape[1]
    features = tokens.shape[2]
    groups = lax.axis_size("wa")
    sequence_total = lax.axis_size("ctx") * local_row_count
    query_group_width = QUERY_HEADS // KEY_VALUE_HEADS
    score_scale = HEAD_SIZE ** (-0.5)
    gathered_weights = (
        lax.all_gather(query_weight, "wa", axis=0, tiled=True),
        lax.all_gather(key_projection_matrix, "wa", axis=0, tiled=True),
        lax.all_gather(value_projection_matrix, "wa", axis=0, tiled=True),
        lax.all_gather(output_weight, "wa", axis=0, tiled=True),
        lax.all_gather(attn_gain, "wa", axis=0, tiled=True),
        lax.all_gather(moe_gain, "wa", axis=0, tiled=True),
        lax.all_gather(router_weight, "wa", axis=0, tiled=True),
        lax.all_gather(shared_gate, "wa", axis=0, tiled=True),
        lax.all_gather(shared_up, "wa", axis=0, tiled=True),
        lax.all_gather(shared_down, "wa", axis=0, tiled=True),
    )
    (
        wq_full,
        wk_full,
        wv_full,
        wo_full,
        first_norm_scale,
        second_norm_scale,
        router_full,
        sgate_full,
        sup_full,
        sdown_full,
    ) = gathered_weights
    first_norm_scale = first_norm_scale.astype(jnp.float32)
    second_norm_scale = second_norm_scale.astype(jnp.float32)
    length = jnp.sum(jnp.where(jnp.arange(lengths.shape[0]) == seq_index, lengths, 0))
    count = jnp.sum(lengths).astype(jnp.float32)
    query_start = block_index * local_row_count
    query_pos = query_start + jnp.arange(local_row_count)
    query_last = query_start + local_row_count - 1
    input_rows = tokens[0].astype(jnp.float32)
    normed_a, factor_a = norm_forward(input_rows, first_norm_scale)
    attn_in = normed_a.astype(jnp.bfloat16)
    query_rows = jnp.dot(attn_in, wq_full, preferred_element_type=jnp.float32).astype(jnp.bfloat16)
    keys_here = jnp.dot(attn_in, wk_full, preferred_element_type=jnp.float32).astype(jnp.bfloat16)
    values_here = jnp.dot(attn_in, wv_full, preferred_element_type=jnp.float32).astype(jnp.bfloat16)
    query_head_rows = query_rows.reshape(
        local_row_count, KEY_VALUE_HEADS, query_group_width, HEAD_SIZE
    )
    local_key_heads = keys_here.reshape(local_row_count, KEY_VALUE_HEADS, HEAD_SIZE)
    local_value_heads = values_here.reshape(local_row_count, KEY_VALUE_HEADS, HEAD_SIZE)

    def key_mask(key_start, key_count_total):
        key_pos = key_start + jnp.arange(key_count_total)
        return (key_pos[None, :] <= query_pos[:, None]) & (key_pos[None, :] < length)

    def sweep(step_fn, carry, pieces):
        key_piece, value_piece = pieces
        key_count_total = key_piece.shape[0]
        size_now = inner_size(key_count_total)

        def sweep_visit(current, offset):
            key_block_tile = lax.dynamic_slice_in_dim(key_piece, offset, size_now, 0)
            value_block_tile = lax.dynamic_slice_in_dim(value_piece, offset, size_now, 0)
            key_begin = offset
            needed = (key_begin <= query_last) & (key_begin < length)
            current = lax.cond(
                needed,
                lambda held: step_fn(held, key_block_tile, value_block_tile, key_begin),
                lambda held: held,
                current,
            )
            return (current, None)

        carry, _ = lax.scan(sweep_visit, carry, jnp.arange(0, key_count_total, size_now))
        return carry

    def forward_step(carry, key_block_tile, value_block_tile, key_begin):
        maxima, totals, accum = carry
        key_count_total = key_block_tile.shape[0]
        key_head_rows = key_block_tile.reshape(key_count_total, KEY_VALUE_HEADS, HEAD_SIZE)
        value_head_rows = value_block_tile.reshape(key_count_total, KEY_VALUE_HEADS, HEAD_SIZE)
        scores = (
            jnp.einsum(
                "tkgd,nkd->kgtn", query_head_rows, key_head_rows, preferred_element_type=jnp.float32
            )
            * score_scale
        )
        allowed = key_mask(key_begin, key_count_total)
        scores = jnp.where(allowed, scores, score_after_mask)
        new_max = jnp.maximum(maxima, jnp.max(scores, axis=-1))
        weights = jnp.where(allowed, jnp.exp(scores - new_max[..., None]), 0.0)
        shrink = jnp.exp(maxima - new_max)
        totals = totals * shrink + jnp.sum(weights, axis=-1)
        update = jnp.einsum(
            "kgtn,nkd->tkgd",
            weights.astype(jnp.bfloat16),
            value_head_rows,
            preferred_element_type=jnp.float32,
        )
        accum = accum * jnp.transpose(shrink, (2, 0, 1))[..., None] + update
        return (new_max, totals, accum)

    init_forward = (
        jnp.full(
            (KEY_VALUE_HEADS, query_group_width, local_row_count), score_after_mask, jnp.float32
        ),
        jnp.zeros((KEY_VALUE_HEADS, query_group_width, local_row_count), jnp.float32),
        jnp.zeros((local_row_count, KEY_VALUE_HEADS, query_group_width, HEAD_SIZE), jnp.float32),
    )
    maxima, totals, accum = sweep(
        forward_step,
        init_forward,
        (
            lax.all_gather(keys_here, "ctx", axis=0, tiled=True),
            lax.all_gather(values_here, "ctx", axis=0, tiled=True),
        ),
    )
    attn_full = accum / jnp.transpose(totals, (2, 0, 1))[..., None]
    log_total = maxima + jnp.log(totals)
    attn_out = attn_full.reshape(local_row_count, QUERY_HEADS * HEAD_SIZE).astype(jnp.bfloat16)
    branch_attn = jnp.einsum("tj,dj->td", attn_out, wo_full, preferred_element_type=jnp.float32)
    resid = input_rows + branch_attn
    normed_b, factor_b = norm_forward(resid, second_norm_scale)
    moe_in = normed_b.astype(jnp.bfloat16)
    logits = jnp.dot(moe_in, router_full, preferred_element_type=jnp.float32)
    experts_all = router_full.shape[1]
    route_ids = routes[0]
    route_hot = (route_ids[:, :, None] == jnp.arange(experts_all)[None, None, :]).astype(
        jnp.float32
    )
    chosen = jnp.sum(route_hot * logits[:, None, :], axis=-1)
    gates = jax.nn.softmax(chosen, axis=-1)
    exp_here = expert_gate.shape[0]
    capacity = 2 * local_row_count * TOP // experts_all
    flat_ids = route_ids.reshape(-1)
    pair_count = flat_ids.shape[0]
    hot_ids = (flat_ids[:, None] == jnp.arange(experts_all)[None, :]).astype(jnp.int32)
    ranks = jnp.sum((jnp.cumsum(hot_ids, axis=0) - hot_ids) * hot_ids, axis=-1)
    dest = flat_ids * capacity + ranks
    slot_pair = (
        jnp.zeros((experts_all * capacity,), jnp.int32)
        .at[dest]
        .set(jnp.arange(pair_count, dtype=jnp.int32))
    )
    slot_live = jnp.zeros((experts_all * capacity,), jnp.bfloat16).at[dest].set(1.0)
    send_rows = (moe_in[slot_pair // TOP] * slot_live[:, None]).reshape(
        groups, exp_here, capacity, features
    )
    recv_rows = lax.all_to_all(send_rows, "wa", split_axis=0, concat_axis=0, tiled=True)
    gate_pre = jnp.einsum(
        "secd,edf->secf", recv_rows, expert_gate, preferred_element_type=jnp.float32
    )
    up_pre = jnp.einsum("secd,edf->secf", recv_rows, expert_up, preferred_element_type=jnp.float32)
    gate_act, gate_slope = silu_parts(gate_pre)
    expert_hidden = (gate_act * up_pre).astype(jnp.bfloat16)
    expert_result = jnp.einsum(
        "secf,edf->secd", expert_hidden, expert_down, preferred_element_type=jnp.float32
    ).astype(jnp.bfloat16)
    returned = lax.all_to_all(expert_result, "wa", split_axis=0, concat_axis=0, tiled=True).reshape(
        experts_all * capacity, features
    )
    pair_out = returned[dest].astype(jnp.float32).reshape(local_row_count, TOP, features)
    moe_out = jnp.sum(gates[:, :, None] * pair_out, axis=1)
    shared_pre = jnp.dot(moe_in, sgate_full, preferred_element_type=jnp.float32)
    shared_lin = jnp.dot(moe_in, sup_full, preferred_element_type=jnp.float32)
    shared_act, shared_slope = silu_parts(shared_pre)
    shared_hidden = (shared_act * shared_lin).astype(jnp.bfloat16)
    shared_out = jnp.einsum(
        "tf,df->td", shared_hidden, sdown_full, preferred_element_type=jnp.float32
    )
    result = resid + moe_out + shared_out
    block_out = result.astype(jnp.bfloat16)
    valid = (query_pos < length).astype(jnp.float32)
    error = result - teacher[0]
    total_loss = lax.psum(jnp.sum(valid[:, None] * error * error), ("ctx", "wa"))
    loss = total_loss / (2.0 * features * count)
    grad_result = error * valid[:, None] * (lengths.shape[0] * sequence_total / count)
    grad_shared_out = grad_result.astype(jnp.bfloat16)
    grad_shared_hidden = jnp.dot(grad_shared_out, sdown_full, preferred_element_type=jnp.float32)
    grad_sdown = jnp.einsum(
        "td,tf->df", grad_shared_out, shared_hidden, preferred_element_type=jnp.float32
    )
    grad_shared_pre = (grad_shared_hidden * shared_lin * shared_slope).astype(jnp.bfloat16)
    grad_shared_lin = (grad_shared_hidden * shared_act).astype(jnp.bfloat16)
    grad_sgate = jnp.einsum(
        "td,tf->df", moe_in, grad_shared_pre, preferred_element_type=jnp.float32
    )
    grad_sup = jnp.einsum("td,tf->df", moe_in, grad_shared_lin, preferred_element_type=jnp.float32)
    grad_moe_in = jnp.einsum(
        "tf,df->td", grad_shared_pre, sgate_full, preferred_element_type=jnp.float32
    )
    grad_moe_in = grad_moe_in + jnp.einsum(
        "tf,df->td", grad_shared_lin, sup_full, preferred_element_type=jnp.float32
    )
    grad_pairs = (
        (gates[:, :, None] * grad_result[:, None, :])
        .astype(jnp.bfloat16)
        .reshape(pair_count, features)
    )
    grad_gates = jnp.sum(pair_out * grad_result[:, None, :], axis=-1)
    grad_send = (grad_pairs[slot_pair] * slot_live[:, None]).reshape(
        groups, exp_here, capacity, features
    )
    grad_recv = lax.all_to_all(grad_send, "wa", split_axis=0, concat_axis=0, tiled=True)
    grad_hidden = jnp.einsum(
        "secd,edf->secf", grad_recv, expert_down, preferred_element_type=jnp.float32
    )
    grad_edown = jnp.einsum(
        "secd,secf->edf", grad_recv, expert_hidden, preferred_element_type=jnp.float32
    )
    grad_gate_pre = (grad_hidden * up_pre * gate_slope).astype(jnp.bfloat16)
    grad_up_pre = (grad_hidden * gate_act).astype(jnp.bfloat16)
    grad_egate = jnp.einsum(
        "secd,secf->edf", recv_rows, grad_gate_pre, preferred_element_type=jnp.float32
    )
    expert_up_gradient = jnp.einsum(
        "secd,secf->edf", recv_rows, grad_up_pre, preferred_element_type=jnp.float32
    )
    grad_rows = jnp.einsum(
        "secf,edf->secd", grad_gate_pre, expert_gate, preferred_element_type=jnp.float32
    )
    grad_rows = (
        grad_rows
        + jnp.einsum("secf,edf->secd", grad_up_pre, expert_up, preferred_element_type=jnp.float32)
    ).astype(jnp.bfloat16)
    grad_back = lax.all_to_all(grad_rows, "wa", split_axis=0, concat_axis=0, tiled=True).reshape(
        experts_all * capacity, features
    )
    grad_moe_in = grad_moe_in + jnp.sum(
        grad_back[dest].astype(jnp.float32).reshape(local_row_count, TOP, features), axis=1
    )
    expert_summed = (
        lax.psum_scatter(grad_egate, "ctx", scatter_dimension=1, tiled=True),
        lax.psum_scatter(expert_up_gradient, "ctx", scatter_dimension=1, tiled=True),
        lax.psum_scatter(grad_edown, "ctx", scatter_dimension=1, tiled=True),
    )
    grad_chosen = gates * (grad_gates - jnp.sum(gates * grad_gates, axis=-1, keepdims=True))
    grad_logits = jnp.sum(route_hot * grad_chosen[:, :, None], axis=1)
    router_float = router_full.astype(jnp.float32)
    grad_router = jnp.dot(moe_in.astype(jnp.float32).T, grad_logits, precision=highest)
    grad_moe_in = grad_moe_in + jnp.dot(grad_logits, router_float.T, precision=highest)
    grad_resid_norm, grad_gain_two = norm_backward(resid, factor_b, second_norm_scale, grad_moe_in)
    grad_resid = grad_result + grad_resid_norm
    grad_branch = grad_resid.astype(jnp.bfloat16)
    grad_wo = jnp.einsum("td,tj->dj", grad_branch, attn_out, preferred_element_type=jnp.float32)
    attention_gradient = jnp.dot(grad_branch, wo_full, preferred_element_type=jnp.float32).astype(
        jnp.bfloat16
    )
    head_gradient_rows = attention_gradient.reshape(
        local_row_count, KEY_VALUE_HEADS, query_group_width, HEAD_SIZE
    )
    delta_rows = jnp.sum(head_gradient_rows.astype(jnp.float32) * attn_full, axis=-1)
    delta = jnp.transpose(delta_rows, (1, 2, 0))

    def backward_step(grad_queries, key_block_tile, value_block_tile, key_begin):
        key_count_total = key_block_tile.shape[0]
        key_head_rows = key_block_tile.reshape(key_count_total, KEY_VALUE_HEADS, HEAD_SIZE)
        value_head_rows = value_block_tile.reshape(key_count_total, KEY_VALUE_HEADS, HEAD_SIZE)
        scores = (
            jnp.einsum(
                "tkgd,nkd->kgtn", query_head_rows, key_head_rows, preferred_element_type=jnp.float32
            )
            * score_scale
        )
        allowed = key_mask(key_begin, key_count_total)
        probs = jnp.where(allowed, jnp.exp(scores - log_total[..., None]), 0.0)
        grad_probs = jnp.einsum(
            "tkgd,nkd->kgtn",
            head_gradient_rows,
            value_head_rows,
            preferred_element_type=jnp.float32,
        )
        grad_scores = (probs * (grad_probs - delta[..., None])).astype(jnp.bfloat16)
        return (
            grad_queries
            + jnp.einsum(
                "kgtn,nkd->tkgd", grad_scores, key_head_rows, preferred_element_type=jnp.float32
            )
            * score_scale
        )

    init_back = jnp.zeros(
        (local_row_count, KEY_VALUE_HEADS, query_group_width, HEAD_SIZE), jnp.float32
    )
    grad_queries = sweep(
        backward_step,
        init_back,
        (
            lax.all_gather(keys_here, "ctx", axis=0, tiled=True),
            lax.all_gather(values_here, "ctx", axis=0, tiled=True),
        ),
    )
    key_pos_here = query_start + jnp.arange(local_row_count)
    init_keys = (
        jnp.zeros((local_row_count, KEY_VALUE_HEADS, HEAD_SIZE), jnp.float32),
        jnp.zeros((local_row_count, KEY_VALUE_HEADS, HEAD_SIZE), jnp.float32),
    )
    query_wide = query_rows.astype(jnp.float32)
    grad_wide = attention_gradient.astype(jnp.float32)
    total_rows = jnp.transpose(log_total, (2, 0, 1))
    key_grads = init_keys
    query_piece = lax.all_gather(query_wide.astype(jnp.bfloat16), "ctx", axis=0, tiled=True).astype(
        jnp.float32
    )
    grad_piece = lax.all_gather(grad_wide.astype(jnp.bfloat16), "ctx", axis=0, tiled=True).astype(
        jnp.float32
    )
    total_piece = lax.all_gather(total_rows.astype(jnp.bfloat16), "ctx", axis=0, tiled=True).astype(
        jnp.float32
    )
    delta_piece = lax.all_gather(delta_rows.astype(jnp.bfloat16), "ctx", axis=0, tiled=True).astype(
        jnp.float32
    )
    piece_rows = query_piece.shape[0]
    size_now = inner_size(piece_rows)

    def key_visit(current, offset):
        query_tile = (
            lax.dynamic_slice_in_dim(query_piece, offset, size_now, 0)
            .astype(jnp.bfloat16)
            .reshape(size_now, KEY_VALUE_HEADS, query_group_width, HEAD_SIZE)
        )
        grad_tile = (
            lax.dynamic_slice_in_dim(grad_piece, offset, size_now, 0)
            .astype(jnp.bfloat16)
            .reshape(size_now, KEY_VALUE_HEADS, query_group_width, HEAD_SIZE)
        )
        total_tile = jnp.transpose(
            lax.dynamic_slice_in_dim(total_piece, offset, size_now, 0), (1, 2, 0)
        )
        delta_tile = jnp.transpose(
            lax.dynamic_slice_in_dim(delta_piece, offset, size_now, 0), (1, 2, 0)
        )
        query_begin = offset

        def add_terms(held):
            tile_pos = query_begin + jnp.arange(size_now)
            allowed = (key_pos_here[None, :] <= tile_pos[:, None]) & (
                key_pos_here[None, :] < length
            )
            scores = (
                jnp.einsum(
                    "tkgd,nkd->kgtn",
                    query_tile,
                    local_key_heads,
                    preferred_element_type=jnp.float32,
                )
                * score_scale
            )
            probs = jnp.where(allowed, jnp.exp(scores - total_tile[..., None]), 0.0)
            grad_probs = jnp.einsum(
                "tkgd,nkd->kgtn", grad_tile, local_value_heads, preferred_element_type=jnp.float32
            )
            grad_scores = (probs * (grad_probs - delta_tile[..., None])).astype(jnp.bfloat16)
            key_gradient_rows = (
                jnp.einsum(
                    "kgtn,tkgd->nkd", grad_scores, query_tile, preferred_element_type=jnp.float32
                )
                * score_scale
            )
            value_gradient_rows = jnp.einsum(
                "kgtn,tkgd->nkd",
                probs.astype(jnp.bfloat16),
                grad_tile,
                preferred_element_type=jnp.float32,
            )
            return (held[0] + key_gradient_rows, held[1] + value_gradient_rows)

        needed = (query_begin + size_now - 1 >= query_start) & (query_start < length)
        current = lax.cond(needed, add_terms, lambda held: held, current)
        return (current, None)

    key_grads, _ = lax.scan(key_visit, key_grads, jnp.arange(0, piece_rows, size_now))
    key_gradient_sum, value_gradient_sum = key_grads
    key_gradient_reduced = key_gradient_sum.reshape(
        local_row_count, KEY_VALUE_HEADS * HEAD_SIZE
    ).astype(jnp.bfloat16)
    value_gradient_reduced = value_gradient_sum.reshape(
        local_row_count, KEY_VALUE_HEADS * HEAD_SIZE
    ).astype(jnp.bfloat16)
    grad_queries_low = grad_queries.reshape(local_row_count, QUERY_HEADS * HEAD_SIZE).astype(
        jnp.bfloat16
    )
    grad_wq = jnp.einsum("td,tj->dj", attn_in, grad_queries_low, preferred_element_type=jnp.float32)
    grad_wk = jnp.einsum(
        "td,tj->dj", attn_in, key_gradient_reduced, preferred_element_type=jnp.float32
    )
    grad_wv = jnp.einsum(
        "td,tj->dj", attn_in, value_gradient_reduced, preferred_element_type=jnp.float32
    )
    grad_attn_in = jnp.einsum(
        "tj,dj->td", grad_queries_low, wq_full, preferred_element_type=jnp.float32
    )
    grad_attn_in = grad_attn_in + jnp.einsum(
        "tj,dj->td", key_gradient_reduced, wk_full, preferred_element_type=jnp.float32
    )
    grad_attn_in = grad_attn_in + jnp.einsum(
        "tj,dj->td", value_gradient_reduced, wv_full, preferred_element_type=jnp.float32
    )
    grad_inputs_norm, grad_gain_one = norm_backward(
        input_rows, factor_a, first_norm_scale, grad_attn_in
    )
    grad_inputs = grad_resid + grad_inputs_norm
    dense_summed = (
        lax.psum_scatter(grad_wq, ("ctx", "wa"), scatter_dimension=0, tiled=True),
        lax.psum_scatter(grad_wk, ("ctx", "wa"), scatter_dimension=0, tiled=True),
        lax.psum_scatter(grad_wv, ("ctx", "wa"), scatter_dimension=0, tiled=True),
        lax.psum_scatter(grad_wo, ("ctx", "wa"), scatter_dimension=0, tiled=True),
        lax.psum_scatter(grad_gain_one, ("ctx", "wa"), scatter_dimension=0, tiled=True),
        lax.psum_scatter(grad_gain_two, ("ctx", "wa"), scatter_dimension=0, tiled=True),
        lax.psum_scatter(grad_router, ("ctx", "wa"), scatter_dimension=0, tiled=True),
        lax.psum_scatter(grad_sgate, ("ctx", "wa"), scatter_dimension=0, tiled=True),
        lax.psum_scatter(grad_sup, ("ctx", "wa"), scatter_dimension=0, tiled=True),
        lax.psum_scatter(grad_sdown, ("ctx", "wa"), scatter_dimension=0, tiled=True),
    )
    return (
        block_out[None],
        grad_inputs[None],
        dense_summed[0],
        dense_summed[1],
        dense_summed[2],
        dense_summed[3],
        dense_summed[4],
        dense_summed[5],
        dense_summed[6],
        dense_summed[7],
        dense_summed[8],
        dense_summed[9],
        expert_summed[0],
        expert_summed[1],
        expert_summed[2],
        loss,
    )


def solution(mesh):
    return jax.shard_map(
        per_device,
        mesh=mesh,
        in_specs=(
            P("wa", "ctx", None),
            P("wa", "ctx", None),
            P(),
            P("wa", "ctx", None),
            P("wa", None),
            P("wa", None),
            P("wa", None),
            P("wa", None),
            P("wa"),
            P("wa"),
            P("wa", None),
            P("wa", None),
            P("wa", None),
            P("wa", None),
            P("wa", None, None),
            P("wa", None, None),
            P("wa", None, None),
        ),
        out_specs=(
            P("wa", "ctx", None),
            P("wa", "ctx", None),
            P(("ctx", "wa"), None),
            P(("ctx", "wa"), None),
            P(("ctx", "wa"), None),
            P(("ctx", "wa"), None),
            P(("ctx", "wa")),
            P(("ctx", "wa")),
            P(("ctx", "wa"), None),
            P(("ctx", "wa"), None),
            P(("ctx", "wa"), None),
            P(("ctx", "wa"), None),
            P("wa", "ctx", None),
            P("wa", "ctx", None),
            P("wa", "ctx", None),
            P(),
        ),
        check_vma=False,
    )
```

profile of v0, /device:TPU:0, one launch (start us, length us, event | category | flops | bytes accessed | tf_op | source)
XLA Modules:
  0.0 2279.7 jit_solution(1720014957378555155)
XLA Ops:
  9.4 6.1 all-gather
  16.7 15.2 all-gather.20.cloned.1.call-done
  34.7 18.5 all-gather.14.cloned.1.call-done
  59.4 5.2 all-gather.1
  67.0 8.6 scatter_custom_fusion.1
  81.0 14.6 all-gather.22.cloned.1.call-done
  97.9 38.7 %all-gather.16.cloned.1.call-done = bf16[1024,512]{1,0:T(8,128)(2,1)} async-done(((bf16[128,512]{1,0:T(8,128)(2,1)}), bf16[1024,512]{1,0:T(8,128)(2,1)}) %all-gather.16.cloned.1.call-update) | async-done | bytes 1048592 | tf_op jit(solution)/shard_map/all_gather | solution.py:177
  138.8 35.4 %all-gather.18.cloned.1.call-done = bf16[1536,1536]{1,0:T(8,128)(2,1)} async-done(((bf16[384,1536]{1,0:T(8,128)(2,1)}), bf16[1536,1536]{1,0:T(8,128)(2,1)}) %all-gather.18.cloned.1.call-update) | async-done | bytes 4718608 | tf_op jit(solution)/shard_map/all_gather | solution.py:73
  178.4 15.4 while.47
  181.7 8.9 conditional.10
  194.2 18.9 all-gather.24.cloned.1.call-done
  217.4 6.3 gather_fusion
  234.3 76.7 %all-to-all-done = bf16[4,4,96,1536]{3,2,1,0:T(8,128)(2,1)} async-done(((bf16[4,4,96,1536]{3,2,1,0:T(8,128)(2,1)}), bf16[4,4,96,1536]{3,2,1,0:T(8,128)(2,1)}, u32[]{:S(2)}, u32[]{:S(2)}) %all-to-all-start) | async-done | bytes 4718624 | tf_op jit(solution)/shard_map/all_to_all | solution.py:212
  311.0 6.3 fusion.68
  317.3 9.8 fusion.85
  338.5 54.1 %all_gather.58 = bf16[1536,16]{0,1:T(8,128)(2,1)S(1)} all-gather(bf16[384,16]{0,1:T(8,128)(2,1)S(1)} %copy-done.65), channel_id=1, replica_groups=mesh['ctx'=8,'wa'=4] {'wa'}, dimensions={0}, use_global_device_ids=true | all-gather | bytes 61440 | tf_op jit(solution)/shard_map/all_gather | solution.py:79
  400.6 8.9 gather_fusion.1
  414.5 5.1 multiply_reduce_fusion.1
  427.8 6.5 mul.429
  437.0 6.4 gather_fusion.2
  453.8 53.3 %all-to-all-done.2 = bf16[4,4,96,1536]{3,2,1,0:T(8,128)(2,1)} async-done(((bf16[4,4,96,1536]{3,2,1,0:T(8,128)(2,1)}), bf16[4,4,96,1536]{3,2,1,0:T(8,128)(2,1)}, u32[]{:S(2)}, u32[]{:S(2)}) %all-to-all-start.2) | async-done | bytes 4718624 | tf_op jit(solution)/shard_map/all_to_all | solution.py:267
  507.1 9.4 fusion.83
  516.5 10.4 fusion.62
  526.9 8.8 fusion.74
  553.7 43.4 %all-to-all-done.3 = bf16[4,4,96,1536]{3,2,1,0:T(8,128)(2,1)} async-done(((bf16[4,4,96,1536]{3,2,1,0:T(8,128)(2,1)}), bf16[4,4,96,1536]{3,2,1,0:T(8,128)(2,1)}, u32[]{:S(2)}, u32[]{:S(2)}) %all-to-all-start.3) | async-done | bytes 4718624 | tf_op jit(solution)/shard_map/all_to_all | solution.py:289
  597.1 8.2 gather_fusion.3
  637.2 21.1 all_gather.63
  659.3 16.9 all_gather.65
  682.5 51.4 %while.49 = (s32[]{:T(128)}, f32[128,4,128]{2,0,1:T(8,128)}, f32[128,4,128]{2,0,1:T(8,128)}, s32[2]{0:T(128)}, s32[]{:T(128)}, /*index=5*/pred[]{:T(512)}, bf16[...) while((s32[]{:T(128)}, f32[128,4,128]{2,0,1:T(8,128)}, ...), condition=%wide.region_32.33_spmd.clone.clone, body=%wide.region_29.32_spmd.clone.clone.sunk | while | flops 813499136 | bytes 36289192 | solution.py:436
  695.4 12.8 conditional.12
  721.1 12.8 conditional.12
  748.0 18.5 while.48
  751.1 12.4 conditional.11
  767.9 6.0 fusion.142
  775.4 9.5 convolution_bitcast_fusion
  786.3 9.5 convolution_bitcast_fusion.2
  797.2 9.6 convolution_bitcast_fusion.1
  814.3 40.1 %all-reduce.2 = (f32[1536]{0:T(1024)S(1)}, f32[1536]{0:T(1024)S(1)}, f32[]{:T(128)}) all-reduce(f32[1536]{0:T(1024)S(1)} %get-tuple-element.1035, f32[1536]{0:T(1024)S(1)} %copy-done.56, f32[]{:T(128)} %get-tuple-element.1132), channel_id=6, replica_groups=mesh['ctx'=8,'wa'=4] {'ctx','wa'}, use_global_device_ids=true, to_apply=%region_39.40.clone | all-reduce | flops 3073 | bytes 24584
  857.5 42.9 %reduce-scatter.22.cloned.1.call-done = f32[48,1024]{1,0:T(8,128)} async-done(((f32[1536,1024]{1,0:T(8,128)}), f32[48,1024]{1,0:T(8,128)}) %reduce-scatter.22.cloned.1.call-update) | async-done | bytes 196624 | tf_op jit(solution)/shard_map/reduce_scatter | solution.py:475
  900.4 120.9 %reduce-scatter.24.cloned.1.call-done = f32[48,1024]{1,0:T(8,128)} async-done(((f32[1536,1024]{1,0:T(8,128)}), f32[48,1024]{1,0:T(8,128)}) %reduce-scatter.24.cloned.1.call-update) | async-done | bytes 196624 | tf_op jit(solution)/shard_map/reduce_scatter | solution.py:476
  1021.2 119.6 %reduce-scatter.26.cloned.1.call-done = f32[48,1024]{1,0:T(8,128)} async-done(((f32[1536,1024]{1,0:T(8,128)}), f32[48,1024]{1,0:T(8,128)}) %reduce-scatter.26.cloned.1.call-update) | async-done | bytes 196624 | tf_op jit(solution)/shard_map/reduce_scatter | solution.py:477
  1140.9 107.6 %reduce-scatter.18.cloned.1.call-done = f32[48,512]{1,0:T(8,128)} async-done(((f32[1536,512]{1,0:T(8,128)}), f32[48,512]{1,0:T(8,128)}) %reduce-scatter.18.cloned.1.call-update) | async-done | bytes 98320 | tf_op jit(solution)/shard_map/reduce_scatter | solution.py:470
  1248.4 107.3 %reduce-scatter.16.cloned.1.call-done = f32[48,512]{1,0:T(8,128)} async-done(((f32[1536,512]{1,0:T(8,128)}), f32[48,512]{1,0:T(8,128)}) %reduce-scatter.16.cloned.1.call-update) | async-done | bytes 98320 | tf_op jit(solution)/shard_map/reduce_scatter | solution.py:469
  1355.7 141.9 %reduce-scatter.20.cloned.1.call-done = f32[48,1536]{1,0:T(8,128)} async-done(((f32[1536,1536]{1,0:T(8,128)}), f32[48,1536]{1,0:T(8,128)}) %reduce-scatter.20.cloned.1.call-update) | async-done | bytes 294928 | tf_op jit(solution)/shard_map/reduce_scatter | solution.py:471
  1497.6 141.3 %reduce-scatter.14.cloned.1.call-done = f32[48,1536]{1,0:T(8,128)} async-done(((f32[1536,1536]{1,0:T(8,128)}), f32[48,1536]{1,0:T(8,128)}) %reduce-scatter.14.cloned.1.call-update) | async-done | bytes 294928 | tf_op jit(solution)/shard_map/reduce_scatter | solution.py:468
  1638.9 210.6 %reduce-scatter.32.cloned.1.call-done = f32[4,192,512]{2,1,0:T(8,128)} async-done(((f32[4,1536,512]{2,1,0:T(8,128)}), f32[4,192,512]{2,1,0:T(8,128)}) %reduce-scatter.32.cloned.1.call-update) | async-done | bytes 1572880 | tf_op jit(solution)/shard_map/reduce_scatter | solution.py:298
  1849.5 211.0 %reduce-scatter.28.cloned.1.call-done = f32[4,192,512]{2,1,0:T(8,128)} async-done(((f32[4,1536,512]{2,1,0:T(8,128)}), f32[4,192,512]{2,1,0:T(8,128)}) %reduce-scatter.28.cloned.1.call-update) | async-done | bytes 1572880 | tf_op jit(solution)/shard_map/reduce_scatter | solution.py:296
  2060.5 211.0 %reduce-scatter.30.cloned.1.call-done = f32[4,192,512]{2,1,0:T(8,128)} async-done(((f32[4,1536,512]{2,1,0:T(8,128)}), f32[4,192,512]{2,1,0:T(8,128)}) %reduce-scatter.30.cloned.1.call-update) | async-done | bytes 1572880 | tf_op jit(solution)/shard_map/reduce_scatter | solution.py:297
  (377 shorter events, 241.9 us)
Async XLA Ops:
  7.2 46.1 %copy-start.4 = (bf16[1,128,1536]{2,1,0:T(8,128)(2,1)S(1)}, bf16[1,128,1536]{2,1,0:T(8,128)(2,1)}, u32[]{:S(2)}) copy-start(bf16[1,128,1536]{2,1,0:T(8,128)(2,1)} %param.29) | copy-start | bytes 1179652
  7.2 24.8 %all-gather.20.cloned.1.call-start = ((), (), s32[]{:S(2)}) async-start(), calls=%async_computation.18 | async-start | bytes 1966080 | tf_op jit(solution)/shard_map/all_gather | solution.py:75
  7.9 45.3 %all-gather.14.cloned.1.call-start = ((), (), s32[]{:S(2)}) async-start(), calls=%async_computation.15 | async-start | bytes 1966080 | tf_op jit(solution)/shard_map/all_gather | solution.py:74
  8.7 86.9 %all-gather.22.cloned.1.call-start = ((), (), s32[]{:S(2)}) async-start(), calls=%async_computation.19 | async-start | bytes 1179648 | tf_op jit(solution)/shard_map/all_gather | solution.py:178
  15.5 158.7 %copy-start.38 = (f32[1536]{0:T(1024)}, f32[1536]{0:T(1024)S(1)}, u32[]{:S(2)}) copy-start(f32[1536]{0:T(1024)S(1)} %reshape.434) | copy-start | bytes 18436
  16.7 157.5 %copy-start.60 = (f32[128]{0:T(128)}, f32[128]{0:T(128)S(1)}, u32[]{:S(2)}) copy-start(f32[128]{0:T(128)S(1)} %add_rsqrt_fusion.1) | copy-start | bytes 1540
  34.6 24.4 %copy-start.59 = (s32[1,128,6]{1,0,2:T(1,128)S(1)}, s32[1,128,6]{1,0,2:T(1,128)}, u32[]{:S(2)}) copy-start(s32[1,128,6]{1,0,2:T(1,128)} %param.32) | copy-start | bytes 9220
  34.6 24.8 %copy-start.70 = (bf16[384]{0:T(512)(128)(2,1)S(1)}, bf16[384]{0:T(512)(128)(2,1)}, u32[]{:S(2)}) copy-start(bf16[384]{0:T(512)(128)(2,1)} %param.38) | copy-start | bytes 2308
  34.6 45.1 %copy-start.71 = (s32[4]{0:T(128)S(1)}, s32[4]{0:T(128)}, u32[]{:S(2)}) copy-start(s32[4]{0:T(128)} %param.31) | copy-start | bytes 52
  34.7 101.9 %all-gather.16.cloned.1.call-start = ((), (), s32[]{:S(2)}) async-start(), calls=%async_computation.16 | async-start | bytes 1179648 | tf_op jit(solution)/shard_map/all_gather | solution.py:177
  55.7 118.5 %all-gather.18.cloned.1.call-start = ((), (), s32[]{:S(2)}) async-start(), calls=%async_computation.17 | async-start | bytes 5898240 | tf_op jit(solution)/shard_map/all_gather | solution.py:73
  56.3 156.8 %all-gather.24.cloned.1.call-start = ((), (), s32[]{:S(2)}) async-start(), calls=%async_computation.20 | async-start | bytes 5898240 | tf_op jit(solution)/shard_map/all_gather | solution.py:76
  56.9 337.6 %all-gather.26.cloned.1.call-start = ((), (), s32[]{:S(2)}) async-start(), calls=%async_computation.21 | async-start | bytes 3932160 | tf_op jit(solution)/shard_map/all_gather | solution.py:80
  57.7 339.4 %all-gather.28.cloned.1.call-start = ((), (), s32[]{:S(2)}) async-start(), calls=%async_computation.22 | async-start | bytes 3932160 | tf_op jit(solution)/shard_map/all_gather | solution.py:81
  64.6 152.6 %copy-start.48 = (f32[1536]{0:T(1024)}, f32[1536]{0:T(1024)S(1)}, u32[]{:S(2)}) copy-start(f32[1536]{0:T(1024)S(1)} %reshape.435) | copy-start | bytes 18436
  75.8 147.9 %copy-start.52 = (bf16[4,4,96]{2,1,0:T(4,128)(2,1)}, bf16[4,4,96]{2,1,0:T(4,128)(2,1)S(1)}, u32[]{:S(2)}) copy-start(bf16[4,4,96]{2,1,0:T(4,128)(2,1)S(1)} %mul.410) | copy-start | bytes 9220
  193.8 23.4 %copy-start.1 = (bf16[128,4,3,128]{3,0,2,1:T(8,128)(2,1)}, bf16[128,4,3,128]{3,0,2,1:T(8,128)(2,1)S(1)}, u32[]{:S(2)}) copy-start(bf16[128,4,3,128]{3,0,2,1:T(8,128)(2,1)S(1)} %get-tuple-element.1551) | copy-start | bytes 1179652
  194.2 23.0 %copy-start.19 = (bf16[128,4,3,128]{0,3,2,1:T(8,128)(2,1)}, bf16[128,4,3,128]{0,3,2,1:T(8,128)(2,1)S(1)}, u32[]{:S(2)}) copy-start(bf16[128,4,3,128]{0,3,2,1:T(8,128)(2,1)S(1)} %fusion.117) | copy-start | bytes 1179652
  217.2 202.4 %copy-start.7 = (f32[128,1536]{1,0:T(8,128)}, f32[128,1536]{1,0:T(8,128)S(1)}, u32[]{:S(2)}) copy-start(f32[128,1536]{1,0:T(8,128)S(1)} %get-tuple-element.1140) | copy-start | bytes 2359300
  228.6 82.4 %all-to-all-start = ((bf16[4,4,96,1536]{3,2,1,0:T(8,128)(2,1)}), bf16[4,4,96,1536]{3,2,1,0:T(8,128)(2,1)}, u32[]{:S(2)}, u32[]{:S(2)}) async-start(bf16[4,4,96,1536]{3,2,1,0:T(8,128)(2,1)} %broadcast_multiply_fusion.1), calls=%async_computation | async-start | bytes 9437184 | tf_op jit(solution)/shard_map/all_to_all | solution.py:212
  233.5 186.1 %all-gather.30.cloned.1.call-start = ((), (), s32[]{:S(2)}) async-start(), calls=%async_computation.23 | async-start | bytes 3932160 | tf_op jit(solution)/shard_map/all_gather | solution.py:82
  332.7 67.9 %all-to-all-start.1 = ((bf16[4,4,96,1536]{3,2,1,0:T(8,128)(2,1)}), bf16[4,4,96,1536]{3,2,1,0:T(8,128)(2,1)}, u32[]{:S(2)}, u32[]{:S(2)}) async-start(bf16[4,4,96,1536]{3,2,1,0:T(8,128)(2,1)} %copy.223), calls=%async_computation.1 | async-start | bytes 9437184 | tf_op jit(solution)/shard_map/all_to_all | solution.py:222
  337.8 62.8 %copy-start.54 = (s32[1,128,6]{1,2,0:T(8,128)}, s32[1,128,6]{1,2,0:T(8,128)S(1)}, u32[]{:S(2)}) copy-start(s32[1,128,6]{1,2,0:T(8,128)S(1)} %copy.300) | copy-start | bytes 9220
  400.6 19.1 copy-start.32
  448.3 58.8 %all-to-all-start.2 = ((bf16[4,4,96,1536]{3,2,1,0:T(8,128)(2,1)}), bf16[4,4,96,1536]{3,2,1,0:T(8,128)(2,1)}, u32[]{:S(2)}, u32[]{:S(2)}) async-start(bf16[4,4,96,1536]{3,2,1,0:T(8,128)(2,1)} %broadcast_multiply_fusion), calls=%async_computation.2 | async-start | bytes 9437184 | tf_op jit(solution)/shard_map/all_to_all | solution.py:267
  453.2 223.7 %all-gather.32.cloned.1.call-start = ((), (), s32[]{:S(2)}) async-start(), calls=%async_computation.24 | async-start | bytes 3538944 | tf_op jit(solution)/shard_map/all_gather | solution.py:365
  538.3 58.8 %all-to-all-start.3 = ((bf16[4,4,96,1536]{3,2,1,0:T(8,128)(2,1)}), bf16[4,4,96,1536]{3,2,1,0:T(8,128)(2,1)}, u32[]{:S(2)}, u32[]{:S(2)}) async-start(bf16[4,4,96,1536]{3,2,1,0:T(8,128)(2,1)} %copy.226), calls=%async_computation.3 | async-start | bytes 9437184 | tf_op jit(solution)/shard_map/all_to_all | solution.py:289
  543.3 137.7 %all-gather.34.cloned.1.call-start = ((), (), s32[]{:S(2)}) async-start(), calls=%async_computation.25 | async-start | bytes 3538944 | tf_op jit(solution)/shard_map/all_gather | solution.py:368
  551.6 45.5 %copy-start.35 = (bf16[128,1024]{1,0:T(8,128)(2,1)}, bf16[128,1024]{1,0:T(8,128)(2,1)S(1)}, u32[]{:S(2)}) copy-start(bf16[128,1024]{1,0:T(8,128)(2,1)S(1)} %get-tuple-element.1135) | copy-start | bytes 786436
  619.9 187.0 %reduce-scatter.34.cloned.1.call-start = ((), (), s32[]{:S(2)}) async-start(), calls=%async_computation.36 | async-start | bytes 811008
  621.4 279.0 %reduce-scatter.22.cloned.1.call-start = ((), (), s32[]{:S(2)}) async-start(), calls=%async_computation.30 | async-start | bytes 6488064 | tf_op jit(solution)/shard_map/reduce_scatter | solution.py:475
  625.2 396.1 %reduce-scatter.24.cloned.1.call-start = ((), (), s32[]{:S(2)}) async-start(), calls=%async_computation.31 | async-start | bytes 6488064 | tf_op jit(solution)/shard_map/reduce_scatter | solution.py:476
  629.8 511.1 %reduce-scatter.26.cloned.1.call-start = ((), (), s32[]{:S(2)}) async-start(), calls=%async_computation.32 | async-start | bytes 6488064 | tf_op jit(solution)/shard_map/reduce_scatter | solution.py:477
  634.4 24.6 %copy-start.16 = (bf16[128,1536]{1,0:T(8,128)(2,1)S(1)}, bf16[128,1536]{1,0:T(8,128)(2,1)}, u32[]{:S(2)}) copy-start(bf16[128,1536]{1,0:T(8,128)(2,1)} %convolution_convert_fusion) | copy-start | bytes 1179652
  634.4 24.8 %copy-start.14 = (f32[128,4,3,128]{0,3,2,1:T(8,128)S(1)}, f32[128,4,3,128]{0,3,2,1:T(8,128)}, u32[]{:S(2)}) copy-start(f32[128,4,3,128]{0,3,2,1:T(8,128)} %copy-done.13) | copy-start | bytes 2359300
  634.4 614.1 %reduce-scatter.18.cloned.1.call-start = ((), (), s32[]{:S(2)}) async-start(), calls=%async_computation.28 | async-start | bytes 3244032 | tf_op jit(solution)/shard_map/reduce_scatter | solution.py:470
  659.2 23.3 %copy-start.17 = (bf16[128,1536]{0,1:T(8,128)(2,1)}, bf16[128,1536]{0,1:T(8,128)(2,1)S(1)}, u32[]{:S(2)}) copy-start(bf16[128,1536]{0,1:T(8,128)(2,1)S(1)} %copy.229) | copy-start | bytes 1179652
  659.3 23.1 %copy-start.57 = (f32[128,4,3]{0,2,1:T(4,128)}, f32[128,4,3]{0,2,1:T(4,128)S(1)}, u32[]{:S(2)}) copy-start(f32[128,4,3]{0,2,1:T(4,128)S(1)} %multiply_reduce_fusion.3) | copy-start | bytes 18436
  682.4 52.5 %copy-start.5 = (bf16[1,128,1536]{2,1,0:T(8,128)(2,1)S(1)}, bf16[1,128,1536]{2,1,0:T(8,128)(2,1)}, u32[]{:S(2)}) copy-start(bf16[1,128,1536]{2,1,0:T(8,128)(2,1)} %param.29) | copy-start | bytes 1179652
  682.5 52.5 %copy-start.39 = (f32[1536]{0:T(1024)S(1)}, f32[1536]{0:T(1024)}, u32[]{:S(2)}) copy-start(f32[1536]{0:T(1024)} %copy-done.38) | copy-start | bytes 18436
  682.5 52.6 %copy-start.61 = (f32[128]{0:T(128)S(1)}, f32[128]{0:T(128)}, u32[]{:S(2)}) copy-start(f32[128]{0:T(128)} %copy-done.60) | copy-start | bytes 1540
  737.4 618.3 %reduce-scatter.16.cloned.1.call-start = ((), (), s32[]{:S(2)}) async-start(), calls=%async_computation.27 | async-start | bytes 3244032 | tf_op jit(solution)/shard_map/reduce_scatter | solution.py:469
  740.0 757.6 %reduce-scatter.20.cloned.1.call-start = ((), (), s32[]{:S(2)}) async-start(), calls=%async_computation.29 | async-start | bytes 9732096 | tf_op jit(solution)/shard_map/reduce_scatter | solution.py:471
  745.2 893.7 %reduce-scatter.14.cloned.1.call-start = ((), (), s32[]{:S(2)}) async-start(), calls=%async_computation.26 | async-start | bytes 9732096 | tf_op jit(solution)/shard_map/reduce_scatter | solution.py:468
  774.0 1075.5 %reduce-scatter.32.cloned.1.call-start = ((), (), s32[]{:S(2)}) async-start(), calls=%async_computation.35 | async-start | bytes 14155776 | tf_op jit(solution)/shard_map/reduce_scatter | solution.py:298
  784.9 1275.6 %reduce-scatter.28.cloned.1.call-start = ((), (), s32[]{:S(2)}) async-start(), calls=%async_computation.33 | async-start | bytes 14155776 | tf_op jit(solution)/shard_map/reduce_scatter | solution.py:296
  795.8 1475.7 %reduce-scatter.30.cloned.1.call-start = ((), (), s32[]{:S(2)}) async-start(), calls=%async_computation.34 | async-start | bytes 14155776 | tf_op jit(solution)/shard_map/reduce_scatter | solution.py:297
  812.8 43.5 %copy-start.11 = (f32[128,1536]{1,0:T(8,128)S(1)}, f32[128,1536]{1,0:T(8,128)}, u32[]{:S(2)}) copy-start(f32[128,1536]{1,0:T(8,128)} %copy-done.9) | copy-start | bytes 2359300
  (59 other events, 273.5 us)
Sparse Core Ops, SparseCore 0:
  9.6 22.3 all-gather.19
  33.5 19.6 all-gather.13
  55.4 40.1 all-gather.21
  97.5 38.9 all-gather.15
  137.9 36.2 all-gather.17
  175.6 37.4 all-gather.23
  214.7 33.5 all-gather.25
  249.8 45.7 all-gather.27
  297.2 30.2 all-gather.29
  456.0 61.8 all-gather.31
  620.0 60.9 all-gather.33
  686.0 94.2 reduce-scatter.33
  786.5 113.8 reduce-scatter.21
  907.4 113.8 reduce-scatter.23
  1027.3 113.5 reduce-scatter.25
  1147.6 100.8 reduce-scatter.17
  1255.2 100.4 reduce-scatter.15
  1363.1 134.5 reduce-scatter.19
  1504.1 134.7 reduce-scatter.13
  1643.3 206.1 reduce-scatter.31
  1854.1 206.3 reduce-scatter.27
  2065.1 206.3 reduce-scatter.29
where the time goes:
time: 2290 us; the launch traced here: 2280 us
  waiting for transfers between devices  1740 us (76%)
  matrix products  173 us (8%)
  blocking collectives  143 us (6%)
  local copies, waits for them, and re-layouts  121 us (5%)
  other arithmetic  46 us (2%)
    reduce_scatter x1, waiting for transfers between devices, per_device(): lax.psum_scatter(grad_egate, 'ctx', scatter_dimension=1, tiled=True)  211 us
    reduce_scatter x1, waiting for transfers between devices, per_device(): lax.psum_scatter(expert_up_gradient, 'ctx', scatter_dimension=1, tiled=True)  211 us
    reduce_scatter x1, waiting for transfers between devices, per_device(): lax.psum_scatter(grad_edown, 'ctx', scatter_dimension=1, tiled=True)  211 us
    reduce_scatter x1, waiting for transfers between devices, per_device(): lax.psum_scatter(grad_wo, ('ctx', 'wa'), scatter_dimension=0, tiled=True)  142 us
    reduce_scatter x1, waiting for transfers between devices, per_device(): lax.psum_scatter(grad_wq, ('ctx', 'wa'), scatter_dimension=0, tiled=True)  141 us
    reduce_scatter x1, waiting for transfers between devices, per_device(): lax.psum_scatter(grad_sup, ('ctx', 'wa'), scatter_dimension=0, tiled=True)  121 us
    reduce_scatter x1, waiting for transfers between devices, per_device(): lax.psum_scatter(grad_sdown, ('ctx', 'wa'), scatter_dimension=0, tiled=True)  120 us
    reduce_scatter x1, waiting for transfers between devices, per_device(): lax.psum_scatter(grad_wv, ('ctx', 'wa'), scatter_dimension=0, tiled=True)  108 us
  transfers between devices with their start and end apart: 26, of which 20 were waited for; matrix products, arithmetic and copies ran while one was open for 13% of the time, Pallas kernels for 0%

commit v1 on v0

v1 whole, which is shorter than its diff:
```python
import jax
import jax.numpy as jnp
from jax import lax
from jax.sharding import PartitionSpec as P

QUERY_HEADS = 12
KEY_VALUE_HEADS = 4
HEAD_SIZE = 128
TOP = 6
GROUP = QUERY_HEADS // KEY_VALUE_HEADS

epsilon = 1e-06
masked = -1e30
bf16 = jnp.bfloat16
f32 = jnp.float32


def dot(a, b, dims):
    return lax.dot_general(a, b, ((dims[0], dims[1]), ((), ())), preferred_element_type=f32)


def mm(a, b):
    return dot(a, b, ((1,), (0,)))


def mm_nt(a, b):
    return dot(a, b, ((1,), (1,)))


def mm_tn(a, b):
    return dot(a, b, ((0,), (0,)))


def swap(value, axis, bit):
    size = lax.axis_size(axis)
    return lax.ppermute(value, axis, [(i, i ^ bit) for i in range(size)])


def perm4(parts, w):
    core, upper = w % 2 == 1, w // 2 == 1
    a, b, c, d = parts
    a, b, c, d = (
        jnp.where(core, b, a),
        jnp.where(core, a, b),
        jnp.where(core, d, c),
        jnp.where(core, c, d),
    )
    return [
        jnp.where(upper, c, a),
        jnp.where(upper, d, b),
        jnp.where(upper, a, c),
        jnp.where(upper, b, d),
    ]


def gather_wa(value):
    near = swap(value, "wa", 1)
    far = swap(value, "wa", 2)
    return [value, near, far, swap(far, "wa", 1)]


def silu_parts(rows):
    sigma = jax.nn.sigmoid(rows)
    return rows * sigma, sigma * (1.0 + rows * (1.0 - sigma))


def rms_factor(rows):
    return lax.rsqrt(jnp.mean(rows * rows, axis=-1, keepdims=True) + epsilon)


def norm_backward(rows, factor, gain, upstream):
    weighted = upstream * gain
    inner = jnp.mean(weighted * rows, axis=-1, keepdims=True)
    grad = factor * weighted - rows * (factor * factor * factor * inner)
    return grad, jnp.sum(upstream * rows * factor, axis=0)


def gather_keys(kv, c, n):
    rows = kv.shape[0]
    if n > 8:
        return lax.all_gather(kv, "ctx", axis=0, tiled=True), jnp.arange(n * rows)
    levels = [kv]
    for s in range(1, n // 2):
        levels.append(lax.ppermute(kv, "ctx", [(i, i + 2 * s) for i in range(n - 2 * s)]))
    blocks, pos = [], []
    for s, level in enumerate(levels):
        blocks += [level, swap(level, "ctx", 1)]
        start = (c - 2 * s) * rows
        pos += [start + jnp.arange(rows), (c - 2 * s + 1 - 2 * (c % 2)) * rows + jnp.arange(rows)]
    return jnp.concatenate(blocks), jnp.concatenate(pos)


def scatter_keys(grads, n):
    rows = grads.shape[0] // n
    if n > 8:
        return lax.psum_scatter(grads, "ctx", scatter_dimension=0, tiled=True).astype(f32)
    blocks = grads.reshape(n, rows, -1)
    total = None
    for s in reversed(range(n // 2)):
        level = blocks[2 * s].astype(f32) + swap(blocks[2 * s + 1], "ctx", 1).astype(f32)
        if s:
            level = lax.ppermute(
                level.astype(bf16), "ctx", [(i + 2 * s, i) for i in range(n - 2 * s)]
            ).astype(f32)
        total = level if total is None else total + level
    return total


def heads(rows, groups):
    return rows.reshape(rows.shape[0], KEY_VALUE_HEADS, groups, HEAD_SIZE)


def attention_scores(q, k, pos, qpos, length):
    scale = HEAD_SIZE**-0.5
    scores = jnp.einsum("tkgd,nkd->kgtn", q, k, preferred_element_type=f32) * scale
    allowed = (pos[None, :] >= 0) & (pos[None, :] <= qpos[:, None]) & (pos[None, :] < length)
    return scores, allowed


def chunked(kv, pos):
    size = 1024
    if kv.shape[0] <= size:
        return None
    return kv.reshape(-1, size, kv.shape[1]), pos.reshape(-1, size)


def attention_forward(q, kv, pos, qpos, length):
    rows = q.shape[0]
    pieces = chunked(kv, pos)
    width = KEY_VALUE_HEADS * HEAD_SIZE
    if pieces is None:
        k, v = heads(kv[:, :width], 1)[:, :, 0], heads(kv[:, width:], 1)[:, :, 0]
        scores, allowed = attention_scores(q, k, pos, qpos, length)
        scores = jnp.where(allowed, scores, masked)
        top = jnp.max(scores, axis=-1, keepdims=True)
        weights = jnp.exp(scores - top)
        probs = (weights / jnp.sum(weights, axis=-1, keepdims=True)).astype(bf16)
        attn = jnp.einsum("kgtn,nkd->tkgd", probs, v, preferred_element_type=f32)
        return attn, probs

    def step(carry, piece):
        top, total, accum = carry
        kv_now, pos_now = piece
        k, v = heads(kv_now[:, :width], 1)[:, :, 0], heads(kv_now[:, width:], 1)[:, :, 0]
        scores, allowed = attention_scores(q, k, pos_now, qpos, length)
        scores = jnp.where(allowed, scores, masked)
        new_top = jnp.maximum(top, jnp.max(scores, axis=-1, keepdims=True))
        weights = jnp.where(allowed, jnp.exp(scores - new_top), 0.0)
        shrink = jnp.exp(top - new_top)
        total = total * shrink + jnp.sum(weights, axis=-1, keepdims=True)
        update = jnp.einsum("kgtn,nkd->kgtd", weights.astype(bf16), v, preferred_element_type=f32)
        return (new_top, total, accum * shrink + update), None

    shape = (KEY_VALUE_HEADS, GROUP, rows)
    start = (
        jnp.full(shape + (1,), masked, f32),
        jnp.zeros(shape + (1,), f32),
        jnp.zeros(shape + (HEAD_SIZE,), f32),
    )
    (top, total, accum), _ = lax.scan(step, start, pieces)
    return jnp.transpose(accum / total, (2, 0, 1, 3)), top + jnp.log(total)


def attention_backward(q, kv, pos, qpos, length, kept, d_attn, delta):
    scale = HEAD_SIZE**-0.5
    width = KEY_VALUE_HEADS * HEAD_SIZE

    def terms(probs, k, v):
        d_probs = jnp.einsum("tkgd,nkd->kgtn", d_attn, v, preferred_element_type=f32)
        d_scores = (probs.astype(f32) * (d_probs - delta)).astype(bf16)
        d_q = jnp.einsum("kgtn,nkd->tkgd", d_scores, k, preferred_element_type=f32) * scale
        d_k = jnp.einsum("kgtn,tkgd->nkd", d_scores, q, preferred_element_type=f32) * scale
        d_v = jnp.einsum(
            "kgtn,tkgd->nkd", probs.astype(bf16), d_attn, preferred_element_type=f32
        )
        keys = k.shape[0]
        return d_q, jnp.concatenate(
            [d_k.reshape(keys, width), d_v.reshape(keys, width)], axis=1
        ).astype(bf16)

    pieces = chunked(kv, pos)
    if pieces is None:
        k, v = heads(kv[:, :width], 1)[:, :, 0], heads(kv[:, width:], 1)[:, :, 0]
        return terms(kept, k, v)

    def step(d_q, piece):
        kv_now, pos_now = piece
        k, v = heads(kv_now[:, :width], 1)[:, :, 0], heads(kv_now[:, width:], 1)[:, :, 0]
        scores, allowed = attention_scores(q, k, pos_now, qpos, length)
        probs = jnp.where(allowed, jnp.exp(scores - kept), 0.0)
        more, d_kv = terms(probs, k, v)
        return d_q + more, d_kv

    d_q, d_kv = lax.scan(step, jnp.zeros(q.shape, f32), pieces)
    return d_q, d_kv.reshape(kv.shape)


def experts_forward(rows, gates, weights):
    e_gate, e_up, e_down, s_gate, s_up, s_down = weights
    out = None
    gate_pres, up_pres, hiddens = [], [], []
    for e in range(e_gate.shape[0]):
        gate_pre, up_pre = mm(rows, e_gate[e]), mm(rows, e_up[e])
        act, _ = silu_parts(gate_pre)
        hidden = (act * up_pre * gates[e]).astype(bf16)
        term = mm_nt(hidden, e_down[e])
        out = term if out is None else out + term
        gate_pres.append(gate_pre.astype(bf16))
        up_pres.append(up_pre.astype(bf16))
        hiddens.append(hidden)
    gate_pre, up_pre = mm(rows, s_gate), mm(rows, s_up)
    act, _ = silu_parts(gate_pre)
    hidden = (act * up_pre).astype(bf16)
    out = out + mm_nt(hidden, s_down)
    kept = (
        jnp.stack(gate_pres),
        jnp.stack(up_pres),
        gate_pre.astype(bf16),
        up_pre.astype(bf16),
    )
    return out, kept, jnp.stack(hiddens), hidden


def experts_backward(grad, gates, weights, kept):
    e_gate, e_up, e_down, s_gate, s_up, s_down = weights
    e_gate_pre, e_up_pre, s_gate_pre, s_up_pre = kept
    d_gates, d_gate_pres, d_up_pres = [], [], []
    d_rows = None
    for e in range(e_gate.shape[0]):
        gate_pre, up_pre = e_gate_pre[e].astype(f32), e_up_pre[e].astype(f32)
        act, slope = silu_parts(gate_pre)
        d_hidden = mm(grad, e_down[e])
        d_gates.append(jnp.sum(d_hidden * act * up_pre, axis=-1))
        d_hidden = d_hidden * gates[e]
        d_gate_pre = (d_hidden * up_pre * slope).astype(bf16)
        d_up_pre = (d_hidden * act).astype(bf16)
        term = mm_nt(d_gate_pre, e_gate[e]) + mm_nt(d_up_pre, e_up[e])
        d_rows = term if d_rows is None else d_rows + term
        d_gate_pres.append(d_gate_pre)
        d_up_pres.append(d_up_pre)
    gate_pre, up_pre = s_gate_pre.astype(f32), s_up_pre.astype(f32)
    act, slope = silu_parts(gate_pre)
    d_hidden = mm(grad, s_down)
    s_d_gate = (d_hidden * up_pre * slope).astype(bf16)
    s_d_up = (d_hidden * act).astype(bf16)
    d_rows = d_rows + mm_nt(s_d_gate, s_gate) + mm_nt(s_d_up, s_up)
    return (
        d_rows,
        jnp.stack(d_gates),
        jnp.stack(d_gate_pres),
        jnp.stack(d_up_pres),
        s_d_gate,
        s_d_up,
    )


def sum_wa(parts):
    own = parts[0] + swap(parts[1].astype(bf16), "wa", 1).astype(f32)
    far = parts[2] + swap(parts[3].astype(bf16), "wa", 1).astype(f32)
    return own + swap(far.astype(bf16), "wa", 2).astype(f32)


def exchange_wa(pick):
    return [pick(0)] + [swap(pick(i), "wa", i) for i in (1, 2, 3)]


def line_scatter(parts, z, n):
    m = n // 2
    if m > 4:
        groups = [[2 * i + x for i in range(m)] for x in range(2)]
        flat = parts.reshape(m, -1)
        done = lax.psum_scatter(
            flat, "ctx", scatter_dimension=0, tiled=True, axis_index_groups=groups
        )
        return done.reshape(parts.shape[1:]).astype(f32)

    def part(index):
        return lax.dynamic_index_in_dim(parts, jnp.clip(index, 0, m - 1), 0, keepdims=False)

    up = down = None
    for t in range(m - 1):
        send_up, send_down = part(z + m - 1 - t), part(z - (m - 1) + t)
        if t:
            send_up = (send_up.astype(f32) + up.astype(f32)).astype(bf16)
            send_down = (send_down.astype(f32) + down.astype(f32)).astype(bf16)
        rising = [(2 * k + x, 2 * k + 2 + x) for k in range(m - 1) if k <= t for x in range(2)]
        falling = [(n - 1 - a, n - 1 - b) for a, b in rising]
        up = lax.ppermute(send_up, "ctx", rising)
        down = lax.ppermute(send_down, "ctx", falling)
    total = part(z).astype(f32)
    if m > 1:
        total = total + up.astype(f32) + down.astype(f32)
    return total


def rows_for(x, value, n):
    m = n // 2
    blocks = value.reshape(m, 2, value.shape[0] // n, value.shape[1])
    return lax.dynamic_index_in_dim(blocks, x, 1, keepdims=False)


def dense_scatter(value, c, n):
    x = c % 2
    value = value.astype(bf16)
    received = swap(rows_for(1 - x, value, n), "ctx", 1)
    mine = (rows_for(x, value, n).astype(f32) + received.astype(f32)).astype(bf16)
    return line_scatter(mine, c // 2, n)


def per_device(
    tokens,
    teacher,
    lengths,
    routes,
    query_weight,
    key_projection_matrix,
    value_projection_matrix,
    output_weight,
    attn_gain,
    moe_gain,
    router_weight,
    shared_gate,
    shared_up,
    shared_down,
    expert_gate,
    expert_up,
    expert_down,
):
    w = lax.axis_index("wa")
    c = lax.axis_index("ctx")
    n = lax.axis_size("ctx")
    groups = lax.axis_size("wa")
    x, z = c % 2, c // 2
    own_tokens = tokens[0]
    rows, features = own_tokens.shape
    slab = features // groups
    length = jnp.sum(jnp.where(jnp.arange(lengths.shape[0]) == w, lengths, 0))
    count = jnp.sum(lengths).astype(f32)
    qpos = c * rows + jnp.arange(rows)

    def columns(value, index):
        return lax.dynamic_slice_in_dim(value, index * slab, slab, 1)

    input_rows = own_tokens.astype(f32)
    factor_a = rms_factor(input_rows)
    far_half = jnp.concatenate([columns(own_tokens, w ^ 2), columns(own_tokens, w ^ 3)], axis=1)
    far_tokens = swap(far_half, "wa", 2)
    far_factor = swap(factor_a, "wa", 2)
    weights_kv = jnp.concatenate([key_projection_matrix, value_projection_matrix], axis=1)
    near_kv = swap(weights_kv, "wa", 1)
    near_q = swap(query_weight, "wa", 1)
    small = jnp.concatenate(
        [router_weight.T, attn_gain[None], moe_gain[None]], axis=0
    )
    near_small = swap(small, "wa", 1)

    gain_own = small[-2:-1].astype(f32)
    gain_near = near_small[-2:-1].astype(f32)
    part_own = jnp.concatenate([columns(own_tokens, w), far_tokens[:, :slab]], axis=0)
    part_near = jnp.concatenate([columns(own_tokens, w ^ 1), far_tokens[:, slab:]], axis=0)
    both_factor = jnp.concatenate([factor_a, far_factor], axis=0)
    normed_own = (part_own.astype(f32) * both_factor * gain_own).astype(bf16)
    normed_near = (part_near.astype(f32) * both_factor * gain_near).astype(bf16)

    def project(weight_own, weight_near):
        partial = mm(normed_own, weight_own) + mm(normed_near, weight_near)
        received = swap(partial[rows:].astype(bf16), "wa", 2)
        return (partial[:rows] + received.astype(f32)).astype(bf16)

    kv = project(weights_kv, near_kv)
    query_rows = project(query_weight, near_q)
    kv_all, pos = gather_keys(kv, c, n)

    far_small = swap(small, "wa", 2)
    smalls = jnp.concatenate(perm4([small, near_small, far_small, swap(far_small, "wa", 1)], w), axis=1)
    router_t = smalls[:-2]
    gain_a, gain_b = smalls[-2].astype(f32), smalls[-1].astype(f32)
    output_parts = gather_wa(output_weight)
    shared_three = jnp.stack([shared_gate, shared_up, shared_down])
    shared_width = shared_three.shape[2] // groups

    def shared_columns(i):
        return lax.dynamic_slice_in_dim(shared_three, (w ^ i) * shared_width, shared_width, 2)

    shared_mine = jnp.concatenate(perm4(exchange_wa(shared_columns), w), axis=1)
    weights = (expert_gate, expert_up, expert_down) + tuple(shared_mine)

    q = heads(query_rows, GROUP)
    attn, kept_attn = attention_forward(q, kv_all, pos, qpos, length)
    attn_out = attn.reshape(rows, -1).astype(bf16)
    branch = jnp.concatenate(perm4([mm_nt(attn_out, part) for part in output_parts], w), axis=1)
    resid = input_rows + branch
    factor_b = rms_factor(resid)
    moe_in = (resid * factor_b * gain_b).astype(bf16)

    experts_all = router_t.shape[0]
    logits = mm_nt(moe_in, router_t)
    chosen = jnp.any(routes[0][:, :, None] == jnp.arange(experts_all), axis=1)
    top = jnp.max(jnp.where(chosen, logits, masked), axis=-1, keepdims=True)
    raised = jnp.where(chosen, jnp.exp(jnp.minimum(logits - top, 0.0)), 0.0)
    gates = raised / jnp.sum(raised, axis=-1, keepdims=True)

    here = expert_gate.shape[0]
    row_parts = gather_wa(moe_in)

    def gates_for(i):
        return lax.dynamic_slice_in_dim(gates.T, (w ^ i) * here, here, 0)

    gate_parts = exchange_wa(gates_for)
    halves = [
        (
            jnp.concatenate(row_parts[2 * h : 2 * h + 2]),
            jnp.concatenate(gate_parts[2 * h : 2 * h + 2], axis=1)[:, :, None],
        )
        for h in range(2)
    ]
    done = [experts_forward(half_rows, half_gates, weights) for half_rows, half_gates in halves]
    out_parts = [done[0][0][:rows], done[0][0][rows:], done[1][0][:rows], done[1][0][rows:]]
    result = resid + sum_wa(out_parts)
    block_out = result.astype(bf16)

    valid = (qpos < length).astype(f32)
    error = (result - teacher[0]) * valid[:, None]
    loss_sum = jnp.sum(error * error)[None]
    grad_result = error * (lengths.shape[0] * n * rows / count)
    grad_low = grad_result.astype(bf16)
    grad_parts = gather_wa(grad_low)

    back = []
    for h in range(2):
        half_grad = jnp.concatenate(grad_parts[2 * h : 2 * h + 2])
        back.append(experts_backward(half_grad, halves[h][1], weights, done[h][1]))
    d_row_parts = [back[0][0][:rows], back[0][0][rows:], back[1][0][:rows], back[1][0][rows:]]
    d_gate_all = jnp.concatenate([back[0][1], back[1][1]], axis=1)
    d_gate_parts = exchange_wa(lambda i: d_gate_all[:, i * rows : (i + 1) * rows])
    grad_moe_in = sum_wa(d_row_parts)
    d_gate = jnp.concatenate(perm4(d_gate_parts, w), axis=0).T
    d_logits = gates * (d_gate - jnp.sum(gates * d_gate, axis=-1, keepdims=True))
    d_logits_low = d_logits.astype(bf16)
    grad_router_t = mm_tn(d_logits_low, moe_in)
    grad_moe_in = grad_moe_in + mm(d_logits_low, router_t)
    grad_norm_b, grad_gain_b = norm_backward(resid, factor_b, gain_b, grad_moe_in)
    grad_resid = grad_result + grad_norm_b
    gz = grad_resid.astype(bf16)

    def fold(expert_value, shared_value):
        half = expert_value.shape[0] // 2
        width = shared_value.shape[1] // 2

        def piece(which):
            return (
                lax.dynamic_slice_in_dim(expert_value, which * half, half, 0),
                lax.dynamic_slice_in_dim(shared_value, which * width, width, 1),
            )

        mine, theirs = piece(x), piece(1 - x)
        got = swap(theirs[0], "ctx", 1), swap(theirs[1], "ctx", 1)
        return (
            jnp.concatenate([mine[0], got[0]], axis=1),
            jnp.concatenate([mine[1], got[1]], axis=0),
        )

    def pair_rows(parts):
        own, far = (
            swap(parts[0], "ctx", 1),
            swap(parts[2], "ctx", 1),
        )
        return jnp.concatenate(parts + [own, swap(own, "wa", 1), far, swap(far, "wa", 1)])

    hidden_all = jnp.concatenate([done[0][2], done[1][2]], axis=1)
    shared_hidden_all = jnp.concatenate([done[0][3], done[1][3]], axis=0)
    rows_pair = pair_rows(row_parts)
    hidden_pair = fold(hidden_all, shared_hidden_all)
    grads_pair = pair_rows(grad_parts)

    def expert_sum(left, pair):
        e_pair, s_pair = pair
        terms = [mm_tn(left, e_pair[e]).astype(bf16) for e in range(e_pair.shape[0])]
        terms.append(mm_tn(left, s_pair).astype(bf16))
        wide = jnp.concatenate(terms, axis=1)
        m = n // 2
        summed = line_scatter(wide.reshape(m, features // m, -1), z, n)
        summed = summed.reshape(2, features // n, -1)
        ours = lax.dynamic_index_in_dim(summed, x, 0, keepdims=False)
        other = lax.dynamic_index_in_dim(summed, 1 - x, 0, keepdims=False)
        got = swap(other.astype(bf16), "ctx", 1).astype(f32)
        first, second = jnp.where(x == 0, ours, got), jnp.where(x == 0, got, ours)
        width = e_pair.shape[2]
        shared = s_pair.shape[1]
        experts = [
            value[:, e * width : (e + 1) * width]
            for value in (first, second)
            for e in range(e_pair.shape[0])
        ]
        shared_columns_sum = jnp.concatenate([first[:, -shared:], second[:, -shared:]], axis=1)
        fine = features // n // groups

        def fine_rows(i):
            return lax.dynamic_slice_in_dim(
                shared_columns_sum.astype(bf16), (w ^ i) * fine, fine, 0
            )

        shared_rows = jnp.concatenate(perm4(exchange_wa(fine_rows), w), axis=1).astype(f32)
        return jnp.stack(experts), shared_rows

    grad_expert_down, grad_shared_down = expert_sum(grads_pair, hidden_pair)
    gate_pair = fold(
        jnp.concatenate([back[0][2], back[1][2]], axis=1),
        jnp.concatenate([back[0][4], back[1][4]], axis=0),
    )
    grad_expert_gate, grad_shared_gate = expert_sum(rows_pair, gate_pair)
    up_pair = fold(
        jnp.concatenate([back[0][3], back[1][3]], axis=1),
        jnp.concatenate([back[0][5], back[1][5]], axis=0),
    )
    grad_expert_up, grad_shared_up = expert_sum(rows_pair, up_pair)

    def fine_columns(value, index):
        blocks = value.reshape(value.shape[0], n, groups, features // n // groups)
        return lax.dynamic_index_in_dim(blocks, index, 2, keepdims=False).reshape(
            value.shape[0], slab
        )

    attn_in = (input_rows * factor_a * gain_a).astype(bf16)
    attn_in_fine = jnp.concatenate(exchange_wa(lambda i: fine_columns(attn_in, w ^ i)))
    attn_out_parts = jnp.concatenate(gather_wa(attn_out))
    gz_fine = jnp.concatenate(exchange_wa(lambda i: fine_columns(gz, w ^ i)))
    grad_output = dense_scatter(mm_tn(gz_fine, attn_out_parts), c, n)

    gz_parts = perm4([columns(gz, s) for s in range(4)], w)
    d_attn_rows = mm(gz_parts[0], output_parts[0])
    for i in range(1, 4):
        d_attn_rows = d_attn_rows + mm(gz_parts[i], output_parts[i])
    d_attn = heads(d_attn_rows.astype(bf16), GROUP)
    delta = jnp.transpose(jnp.sum(d_attn.astype(f32) * attn, axis=-1), (1, 2, 0))[..., None]
    d_q, d_kv_terms = attention_backward(
        q, kv_all, pos, qpos, length, kept_attn, d_attn, delta
    )
    d_q_low = d_q.reshape(rows, -1).astype(bf16)
    far_d_q = swap(d_q_low, "wa", 2)
    d_kv_low = scatter_keys(d_kv_terms, n).astype(bf16)
    far_d_kv = swap(d_kv_low, "wa", 2)

    both_d_q = jnp.concatenate([d_q_low, far_d_q])
    both_d_kv = jnp.concatenate([d_kv_low, far_d_kv])
    all_d_q = jnp.concatenate([d_q_low, swap(d_q_low, "wa", 1), far_d_q, swap(far_d_q, "wa", 1)])
    all_d_kv = jnp.concatenate(
        [d_kv_low, swap(d_kv_low, "wa", 1), far_d_kv, swap(far_d_kv, "wa", 1)]
    )
    grad_query = dense_scatter(mm_tn(attn_in_fine, all_d_q), c, n)

    back_own = mm_nt(both_d_q, query_weight) + mm_nt(both_d_kv, weights_kv)
    back_near = mm_nt(both_d_q, near_q) + mm_nt(both_d_kv, near_kv)
    returned = swap(
        jnp.concatenate([back_own[rows:], back_near[rows:]], axis=1).astype(bf16), "wa", 2
    ).astype(f32)
    grad_attn_in = jnp.concatenate(
        perm4([back_own[:rows], back_near[:rows], returned[:, :slab], returned[:, slab:]], w),
        axis=1,
    )
    grad_norm_a, grad_gain_a = norm_backward(input_rows, factor_a, gain_a, grad_attn_in)
    grad_tokens = grad_resid + grad_norm_a

    smalls_grad = jnp.concatenate(
        [grad_router_t, grad_gain_a[None], grad_gain_b[None]], axis=0
    )
    small_parts = exchange_wa(lambda i: fine_columns(smalls_grad, w ^ i))
    small_sum = (small_parts[0] + small_parts[1] + small_parts[2] + small_parts[3]).T
    kv_and_small = jnp.concatenate([mm_tn(attn_in_fine, all_d_kv), small_sum], axis=1)
    summed = dense_scatter(kv_and_small, c, n)
    width = KEY_VALUE_HEADS * HEAD_SIZE
    grad_key, grad_value = summed[:, :width], summed[:, width : 2 * width]
    grad_router = summed[:, 2 * width : 2 * width + experts_all]
    grad_attn_gain = summed[:, 2 * width + experts_all]
    grad_moe_gain = summed[:, 2 * width + experts_all + 1]

    bit = 1
    while bit < groups:
        loss_sum = loss_sum + swap(loss_sum, "wa", bit)
        bit *= 2
    bit = 1
    while bit < n:
        loss_sum = loss_sum + swap(loss_sum, "ctx", bit)
        bit *= 2
    loss = loss_sum[0] / (2.0 * features * count)

    return (
        block_out[None],
        grad_tokens[None],
        grad_query,
        grad_key,
        grad_value,
        grad_output,
        grad_attn_gain,
        grad_moe_gain,
        grad_router,
        grad_shared_gate,
        grad_shared_up,
        grad_shared_down,
        grad_expert_gate,
        grad_expert_up,
        grad_expert_down,
        loss,
    )


def solution(mesh):
    return jax.shard_map(
        per_device,
        mesh=mesh,
        in_specs=(
            P("wa", "ctx", None),
            P("wa", "ctx", None),
            P(),
            P("wa", "ctx", None),
            P("wa", None),
            P("wa", None),
            P("wa", None),
            P("wa", None),
            P("wa"),
            P("wa"),
            P("wa", None),
            P("wa", None),
            P("wa", None),
            P("wa", None),
            P("wa", None, None),
            P("wa", None, None),
            P("wa", None, None),
        ),
        out_specs=(
            P("wa", "ctx", None),
            P("wa", "ctx", None),
            P(("ctx", "wa"), None),
            P(("ctx", "wa"), None),
            P(("ctx", "wa"), None),
            P(("ctx", "wa"), None),
            P(("ctx", "wa")),
            P(("ctx", "wa")),
            P(("ctx", "wa"), None),
            P(("ctx", "wa"), None),
            P(("ctx", "wa"), None),
            P(("ctx", "wa"), None),
            P("wa", "ctx", None),
            P("wa", "ctx", None),
            P("wa", "ctx", None),
            P(),
        ),
        check_vma=False,
    )
```

time: 2290 us -> 798 us (0.35)
  waiting for transfers between devices: 1740 us -> 208 us
  starting transfers between devices: 22.2 us -> 257 us
  blocking collectives: 143 us -> 0 us
  local copies, waits for them, and re-layouts: 121 us -> 89 us
  other arithmetic: 46 us -> 77.5 us
  matrix products: 173 us -> 144 us
    reduce_scatter x10 -> x0, waiting for transfers between devices: 1410 us -> none  [the longest x1 211 us: per_device(): lax.psum_scatter(grad_egate, 'ctx', scatter_dimension=1, tiled=True)]
    ppermute x0 -> x136, starting transfers between devices: none -> 257 us  [the longest x18 141 us: line_scatter(): up = lax.ppermute(send_up, 'ctx', rising)]
    ppermute x0 -> x136, waiting for transfers between devices: none -> 208 us  [the longest x94 130 us: swap(): return lax.ppermute(value, axis, [(i, i ^ bit) for i in range(size)])]
    all_to_all x4 -> x0, waiting for transfers between devices: 173 us -> none  [the longest x1 76.7 us: per_device(): lax.all_to_all(send_rows, 'wa', split_axis=0, concat_axis=0, tiled=True)]
    all_gather x11 -> x0, waiting for transfers between devices: 146 us -> none  [the longest x1 38.7 us: per_device(): lax.all_gather(keys_here, 'ctx', axis=0, tiled=True)]
    all_gather x5 -> x0, blocking collectives: 103 us -> none  [the longest x1 54.1 us: per_device(): lax.all_gather(router_weight, 'wa', axis=0, tiled=True)]
    unnamed x1 -> x0, blocking collectives: 40.1 us -> none
    dot_general x42 -> x96, matrix products: 172 us -> 139 us  [the longest x91 128 us: dot(): lax.dot_general(a, b, ((dims[0], dims[1]), ((), ())), preferred_element_t...]
  transfers between devices with their start and end apart: 26 -> 136, of which waited for: 20 -> 41; matrix products, arithmetic and copies ran while one was open for 13% -> 37% of each run, Pallas kernels for 0% -> 0%
where the time goes in v1:
time: 798 us; the launch traced here: 786 us
  starting transfers between devices  257 us (32%)
  waiting for transfers between devices  208 us (26%)
  matrix products  144 us (18%)
  local copies, waits for them, and re-layouts  89 us (11%)
  other arithmetic  77.5 us (10%)
  between operations  10.8 us (1%)
    ppermute x18, starting transfers between devices, line_scatter(): up = lax.ppermute(send_up, 'ctx', rising)  141 us
    ppermute x94, waiting for transfers between devices, swap(): return lax.ppermute(value, axis, [(i, i ^ bit) for i in range(size)])  130 us
    dot_general x91, matrix products, dot(): lax.dot_general(a, b, ((dims[0], dims[1]), ((), ())), preferred_element_t...  128 us
    ppermute x94, starting transfers between devices, swap(): return lax.ppermute(value, axis, [(i, i ^ bit) for i in range(size)])  82.4 us
    ppermute x18, waiting for transfers between devices, line_scatter(): up = lax.ppermute(send_up, 'ctx', rising)  40.9 us
    unnamed x360, local copies, waits for them, and re-layouts  20.7 us
    ppermute x3, waiting for transfers between devices, scatter_keys(): lax.ppermute(level.astype(bf16), 'ctx', [(i + 2 * s, i) for i in range(n...  20 us
    ppermute x18, starting transfers between devices, line_scatter(): down = lax.ppermute(send_down, 'ctx', falling)  19.3 us
  transfers between devices with their start and end apart: 136, of which 41 were waited for; matrix products, arithmetic and copies ran while one was open for 37% of the time, Pallas kernels for 0%

profile of v1, /device:TPU:0, one launch (start us, length us, event | category | flops | bytes accessed | tf_op | source)
XLA Modules:
  0.0 786.2 jit_solution(8831355977120232062)
XLA Ops:
  39.3 21.3 %collective-permute-done.4 = bf16[128,1024]{1,0:T(8,128)(2,1)S(1)} collective-permute-done((bf16[128,1024]{1,0:T(8,128)(2,1)S(1)}, bf16[128,1024]{1,0:T(8,128)(2,1)S(1)}, u32[]{:S(2)}, u32[]{:S(2)}) %collective-permute-start.4) | collective-permute-done | bytes 262176 | tf_op jit(solution)/shard_map/ppermute | solution.py:36
  61.3 4.0 collective-permute-start.6
  65.3 3.9 broadcast_select_fusion.7
  70.7 4.5 collective-permute-start.8
  82.5 6.1 collective-permute-done.14
  90.8 6.8 collective-permute-done.11
  105.1 4.9 fusion.443
  110.0 3.4 divide_convert_fusion
  137.2 7.7 collective-permute-done.28
  184.9 12.2 %multiply_convert_fusion.21 = (bf16[256,256]{1,0:T(8,128)(2,1)S(1)}, bf16[256,256]{1,0:T(8,128)(2,1)}) fusion(f32[256,256]{1,0:T(8,128)S(1)} %fusion.287, bf16[256,1536]{1,0:T(8,128)(2,1)S(1)} %get-tuple-element.230, bf16[3,1536,256]{2,1,0:T(8,128)(2,1)S(1)} %copy-done.9), kind=kOutput, calls=%fused_computation.616 | convolution fusion | flops 201785344 | bytes 2097152 | tf_op jit(solution)/shard_map/dot_general | solution.py:19
  207.0 9.4 %collective-permute-done.30 = bf16[128,1536]{1,0:T(8,128)(2,1)S(1)} collective-permute-done((bf16[128,1536]{1,0:T(8,128)(2,1)S(1)}, bf16[128,1536]{1,0:T(8,128)(2,1)S(1)}, u32[]{:S(2)}, u32[]{:S(2)}) %collective-permute-start.30) | collective-permute-done | bytes 393248 | tf_op jit(solution)/shard_map/ppermute | solution.py:36
  227.3 6.7 collective-permute-start.132
  240.0 6.3 collective-permute-start.134
  247.3 4.7 collective-permute-start.135
  299.7 23.8 %collective-permute-done.92 = bf16[512,128]{1,0:T(8,128)(2,1)S(1)} collective-permute-done((bf16[512,128]{1,0:T(8,128)(2,1)S(1)}, bf16[512,128]{1,0:T(8,128)(2,1)S(1)}, u32[]{:S(2)}, u32[]{:S(2)}) %collective-permute-start.92) | collective-permute-done | bytes 131104 | tf_op jit(solution)/shard_map/ppermute | solution.py:36
  337.8 5.9 copy.274
  369.0 3.4 fusion.126
  374.6 4.9 collective-permute-start.121
  392.4 7.3 collective-permute-done.103
  406.4 3.9 copy.272
  410.3 4.4 copy.273
  414.6 4.1 dynamic-slice_bitcast_fusion.5
  429.8 3.6 collective-permute-done.46
  434.4 16.5 %collective-permute-done.44 = bf16[128,1024]{0,1:T(8,128)(2,1)S(1)} collective-permute-done((bf16[128,1024]{0,1:T(8,128)(2,1)S(1)}, bf16[128,1024]{0,1:T(8,128)(2,1)S(1)}, u32[]{:S(2)}, u32[]{:S(2)}) %collective-permute-start.44) | collective-permute-done | bytes 262176 | tf_op jit(solution)/shard_map/ppermute | solution.py:102
  455.0 7.8 collective-permute-done.40
  462.9 5.3 collective-permute-done.48
  480.0 4.4 collective-permute-start.82
  508.6 5.3 collective-permute-start.93
  524.4 5.6 collective-permute-start.122
  533.3 26.3 %collective-permute-start.83 = (bf16[48,1536]{1,0:T(8,128)(2,1)S(1)}, bf16[48,1536]{1,0:T(8,128)(2,1)S(1)}, u32[]{:S(2)}, u32[]{:S(2)}) collective-permute-start(bf16[48,1536]{1,0:T(8,128)(2,1)S(1)} %copy-done.75), channel_id=1, source_target_pairs={{0,8},{4,12},{8,16},{12,20},{16,24},{20,28},{1,9},{5,13},{9,17},{1... | collective-permute-start | bytes 442376 | tf_op jit(solution)/shard_map/ppermute | solution.py:288
  565.8 7.6 collective-permute-done.83
  577.8 8.4 %collective-permute-start.94 = (bf16[384,1152]{1,0:T(8,128)(2,1)}, bf16[384,1152]{1,0:T(8,128)(2,1)}, u32[]{:S(2)}, u32[]{:S(2)}) collective-permute-start(bf16[384,1152]{1,0:T(8,128)(2,1)} %fusion.27), channel_id=1, source_target_pairs={{0,8},{4,12},{8,16},{12,20},{1,9},{5,13},{9,17},{13,21},{2,10},{6,... | collective-permute-start | bytes 2654216 | tf_op jit(solution)/shard_map/ppermute | solution.py:288
  591.4 7.5 collective-permute-done.67
  599.1 6.5 collective-permute-start.68
  609.7 4.4 collective-permute-start.69
  616.6 4.4 collective-permute-start.57
  624.8 4.4 collective-permute-start.70
  632.7 9.5 %collective-permute-start.58 = (bf16[48,1536]{1,0:T(8,128)(2,1)}, bf16[48,1536]{1,0:T(8,128)(2,1)}, u32[]{:S(2)}, u32[]{:S(2)}) collective-permute-start(bf16[48,1536]{1,0:T(8,128)(2,1)} %get-tuple-element.213), channel_id=1, source_target_pairs={{0,8},{4,12},{8,16},{12,20},{16,24},{20,28},{1,9},{5,13},{9,17},{1... | collective-permute-start | bytes 442376 | tf_op jit(solution)/shard_map/ppermute | solution.py:288
  647.8 4.6 collective-permute-start.106
  655.0 3.9 collective-permute-start.123
  662.2 18.3 %collective-permute-start.95 = (bf16[384,1152]{1,0:T(8,128)(2,1)S(1)}, bf16[384,1152]{1,0:T(8,128)(2,1)S(1)}, u32[]{:S(2)}, u32[]{:S(2)}) collective-permute-start(bf16[384,1152]{1,0:T(8,128)(2,1)S(1)} %get-tuple-element.136), channel_id=1, source_target_pairs={{0,8},{4,12},{8,16},{12,20},{16,24},{20,28},{1,9},{5,13},{9,17},{1... | collective-permute-start | bytes 2654216 | tf_op jit(solution)/shard_map/ppermute | solution.py:288
  686.2 5.5 collective-permute-done.123
  691.7 10.4 %collective-permute-done.126 = bf16[384,1152]{1,0:T(8,128)(2,1)S(1)} collective-permute-done((bf16[384,1152]{1,0:T(8,128)(2,1)S(1)}, bf16[384,1152]{1,0:T(8,128)(2,1)S(1)}, u32[]{:S(2)}, u32[]{:S(2)}) %collective-permute-start.126) | collective-permute-done | bytes 884768 | tf_op jit(solution)/shard_map/ppermute | solution.py:289
  703.7 7.2 collective-permute-done.127
  715.0 26.7 %collective-permute-start.107 = (bf16[384,1152]{1,0:T(8,128)(2,1)S(1)}, bf16[384,1152]{1,0:T(8,128)(2,1)S(1)}, u32[]{:S(2)}, u32[]{:S(2)}) collective-permute-start(bf16[384,1152]{1,0:T(8,128)(2,1)S(1)} %get-tuple-element.132), channel_id=1, source_target_pairs={{0,8},{4,12},{8,16},{12,20},{16,24},{20,28},{1,9},{5,13},{9,17},{1... | collective-permute-start | bytes 2654216 | tf_op jit(solution)/shard_map/ppermute | solution.py:288
  745.1 15.4 %collective-permute-done.107 = bf16[384,1152]{1,0:T(8,128)(2,1)S(1)} collective-permute-done((bf16[384,1152]{1,0:T(8,128)(2,1)S(1)}, bf16[384,1152]{1,0:T(8,128)(2,1)S(1)}, u32[]{:S(2)}, u32[]{:S(2)}) %collective-permute-start.107) | collective-permute-done | bytes 884768 | tf_op jit(solution)/shard_map/ppermute | solution.py:288
  760.5 4.2 collective-permute-done.110
  766.2 9.4 %collective-permute-done.111 = bf16[192,1152]{1,0:T(8,128)(2,1)S(1)} collective-permute-done((bf16[192,1152]{1,0:T(8,128)(2,1)S(1)}, bf16[192,1152]{1,0:T(8,128)(2,1)S(1)}, u32[]{:S(2)}, u32[]{:S(2)}) %collective-permute-start.111) | collective-permute-done | bytes 442400 | tf_op jit(solution)/shard_map/ppermute | solution.py:36
  (881 shorter events, 382.8 us)
Async XLA Ops:
  24.7 50.5 %collective-permute-start.12 = (bf16[384,1536]{1,0:T(8,128)(2,1)}, bf16[384,1536]{1,0:T(8,128)(2,1)}, u32[]{:S(2)}, u32[]{:S(2)}) collective-permute-start(bf16[384,1536]{1,0:T(8,128)(2,1)} %param.21), channel_id=1, source_target_pairs={{0,1},{1,0},{2,3},{3,2},{4,5},{5,4},{6,7},{7,6},{8,9},{9,8},{10,11... | collective-permute-start | bytes 3538952 | tf_op jit(solution)/shard_map/ppermute | solution.py:36
  26.4 34.8 %collective-permute-start.21 = (bf16[3,384,256]{2,1,0:T(8,128)(2,1)}, bf16[3,384,256]{2,1,0:T(8,128)(2,1)}, u32[]{:S(2)}, u32[]{:S(2)}) collective-permute-start(bf16[3,384,256]{2,1,0:T(8,128)(2,1)} %get-tuple-element.143), channel_id=1, source_target_pairs={{0,3},{1,2},{2,1},{3,0},{4,7},{5,6},{6,5},{7,4},{8,11},{9,10},{10,... | collective-permute-start | bytes 1769480 | tf_op jit(solution)/shard_map/ppermute | solution.py:36
  27.9 37.4 %collective-permute-start.22 = (bf16[3,384,256]{2,1,0:T(8,128)(2,1)}, bf16[3,384,256]{2,1,0:T(8,128)(2,1)}, u32[]{:S(2)}, u32[]{:S(2)}) collective-permute-start(bf16[3,384,256]{2,1,0:T(8,128)(2,1)} %get-tuple-element.142), channel_id=1, source_target_pairs={{0,2},{1,3},{2,0},{3,1},{4,6},{5,7},{6,4},{7,5},{8,10},{9,11},{10,... | collective-permute-start | bytes 1769480 | tf_op jit(solution)/shard_map/ppermute | solution.py:36
  33.0 32.3 %collective-permute-start.23 = (bf16[3,384,256]{2,1,0:T(8,128)(2,1)}, bf16[3,384,256]{2,1,0:T(8,128)(2,1)S(1)}, u32[]{:S(2)}, u32[]{:S(2)}) collective-permute-start(bf16[3,384,256]{2,1,0:T(8,128)(2,1)} %get-tuple-element.141), channel_id=1, source_target_pairs={{0,1},{1,0},{2,3},{3,2},{4,5},{5,4},{6,7},{7,6},{8,9},{9,8},{10,11... | collective-permute-start | bytes 1769480 | tf_op jit(solution)/shard_map/ppermute | solution.py:36
  60.5 28.1 %collective-permute-start.14 = (bf16[384,1536]{1,0:T(8,128)(2,1)}, bf16[384,1536]{1,0:T(8,128)(2,1)}, u32[]{:S(2)}, u32[]{:S(2)}) collective-permute-start(bf16[384,1536]{1,0:T(8,128)(2,1)} %param.24), channel_id=1, source_target_pairs={{0,2},{1,3},{2,0},{3,1},{4,6},{5,7},{6,4},{7,5},{8,10},{9,11},{10,... | collective-permute-start | bytes 3538952 | tf_op jit(solution)/shard_map/ppermute | solution.py:36
  79.1 45.3 %collective-permute-start.16 = (bf16[384,1536]{1,0:T(8,128)(2,1)}, bf16[384,1536]{1,0:T(8,128)(2,1)}, u32[]{:S(2)}, u32[]{:S(2)}) collective-permute-start(bf16[384,1536]{1,0:T(8,128)(2,1)} %param.24), channel_id=1, source_target_pairs={{0,1},{1,0},{2,3},{3,2},{4,5},{5,4},{6,7},{7,6},{8,9},{9,8},{10,11... | collective-permute-start | bytes 3538952 | tf_op jit(solution)/shard_map/ppermute | solution.py:36
  88.9 37.4 %collective-permute-start.15 = (bf16[384,1536]{1,0:T(8,128)(2,1)}, bf16[384,1536]{1,0:T(8,128)(2,1)}, u32[]{:S(2)}, u32[]{:S(2)}) collective-permute-start(bf16[384,1536]{1,0:T(8,128)(2,1)} %collective-permute-done.14), channel_id=1, source_target_pairs={{0,1},{1,0},{2,3},{3,2},{4,5},{5,4},{6,7},{7,6},{8,9},{9,8},{10,11... | collective-permute-start | bytes 3538952 | tf_op jit(solution)/shard_map/ppermute | solution.py:36
  133.2 239.1 %collective-permute-start.77 = (bf16[128,1536]{0,1:T(8,128)(2,1)}, bf16[128,1536]{0,1:T(8,128)(2,1)}, u32[]{:S(2)}, u32[]{:S(2)}) collective-permute-start(bf16[128,1536]{0,1:T(8,128)(2,1)} %bitcast.13), channel_id=1, source_target_pairs={{0,1},{1,0},{2,3},{3,2},{4,5},{5,4},{6,7},{7,6},{8,9},{9,8},{10,11... | collective-permute-start | bytes 1179656 | tf_op jit(solution)/shard_map/ppermute | solution.py:36
  133.2 240.5 %collective-permute-start.79 = (bf16[128,1536]{0,1:T(8,128)(2,1)}, bf16[128,1536]{0,1:T(8,128)(2,1)}, u32[]{:S(2)}, u32[]{:S(2)}) collective-permute-start(bf16[128,1536]{0,1:T(8,128)(2,1)} %collective-permute-done.78), channel_id=1, source_target_pairs={{0,1},{1,0},{2,3},{3,2},{4,5},{5,4},{6,7},{7,6},{8,9},{9,8},{10,11... | collective-permute-start | bytes 1179656 | tf_op jit(solution)/shard_map/ppermute | solution.py:36
  133.7 42.9 %collective-permute-start.25 = (bf16[128,1536]{1,0:T(8,128)(2,1)S(1)}, bf16[128,1536]{1,0:T(8,128)(2,1)}, u32[]{:S(2)}, u32[]{:S(2)}) collective-permute-start(bf16[128,1536]{1,0:T(8,128)(2,1)S(1)} %get-tuple-element.117), channel_id=1, source_target_pairs={{0,2},{1,3},{2,0},{3,1},{4,6},{5,7},{6,4},{7,5},{8,10},{9,11},{10,... | collective-permute-start | bytes 1179656 | tf_op jit(solution)/shard_map/ppermute | solution.py:36
  146.5 30.6 %collective-permute-start.87 = (bf16[128,1536]{1,0:T(8,128)(2,1)S(1)}, bf16[128,1536]{1,0:T(8,128)(2,1)S(1)}, u32[]{:S(2)}, u32[]{:S(2)}) collective-permute-start(bf16[128,1536]{1,0:T(8,128)(2,1)S(1)} %get-tuple-element.117), channel_id=1, source_target_pairs={{0,4},{4,0},{8,12},{12,8},{16,20},{20,16},{24,28},{28,24},{1,5},{5... | collective-permute-start | bytes 1179656 | tf_op jit(solution)/shard_map/ppermute | solution.py:36
  176.8 27.8 %collective-permute-start.89 = (bf16[128,1536]{1,0:T(8,128)(2,1)}, bf16[128,1536]{1,0:T(8,128)(2,1)S(1)}, u32[]{:S(2)}, u32[]{:S(2)}) collective-permute-start(bf16[128,1536]{1,0:T(8,128)(2,1)} %collective-permute-done.25), channel_id=1, source_target_pairs={{0,4},{4,0},{8,12},{12,8},{16,20},{20,16},{24,28},{28,24},{1,5},{5... | collective-permute-start | bytes 1179656 | tf_op jit(solution)/shard_map/ppermute | solution.py:36
  177.1 27.0 %collective-permute-start.88 = (bf16[128,1536]{1,0:T(8,128)(2,1)S(1)}, bf16[128,1536]{1,0:T(8,128)(2,1)S(1)}, u32[]{:S(2)}, u32[]{:S(2)}) collective-permute-start(bf16[128,1536]{1,0:T(8,128)(2,1)S(1)} %collective-permute-done.87), channel_id=1, source_target_pairs={{0,1},{1,0},{2,3},{3,2},{4,5},{5,4},{6,7},{7,6},{8,9},{9,8},{10,11... | collective-permute-start | bytes 1179656 | tf_op jit(solution)/shard_map/ppermute | solution.py:36
  220.0 34.0 %collective-permute-start.31 = (bf16[128,1536]{1,0:T(8,128)(2,1)}, bf16[128,1536]{1,0:T(8,128)(2,1)S(1)}, u32[]{:S(2)}, u32[]{:S(2)}) collective-permute-start(bf16[128,1536]{1,0:T(8,128)(2,1)} %get-tuple-element.111), channel_id=1, source_target_pairs={{0,1},{1,0},{2,3},{3,2},{4,5},{5,4},{6,7},{7,6},{8,9},{9,8},{10,11... | collective-permute-start | bytes 1179656 | tf_op jit(solution)/shard_map/ppermute | solution.py:36
  223.1 48.9 %collective-permute-start.33 = (bf16[128,1536]{1,0:T(8,128)(2,1)}, bf16[128,1536]{1,0:T(8,128)(2,1)}, u32[]{:S(2)}, u32[]{:S(2)}) collective-permute-start(bf16[128,1536]{1,0:T(8,128)(2,1)} %get-tuple-element.111), channel_id=1, source_target_pairs={{0,2},{1,3},{2,0},{3,1},{4,6},{5,7},{6,4},{7,5},{8,10},{9,11},{10,... | collective-permute-start | bytes 1179656 | tf_op jit(solution)/shard_map/ppermute | solution.py:36
  263.5 31.1 %collective-permute-start.39 = (f32[4,128]{1,0:T(4,128)S(1)}, f32[4,128]{1,0:T(4,128)S(1)}, u32[]{:S(2)}, u32[]{:S(2)}) collective-permute-start(f32[4,128]{1,0:T(4,128)S(1)} %slice.454), channel_id=1, source_target_pairs={{0,1},{1,0},{2,3},{3,2},{4,5},{5,4},{6,7},{7,6},{8,9},{9,8},{10,11... | collective-permute-start | bytes 6152 | tf_op jit(solution)/shard_map/ppermute | solution.py:36
  294.7 34.4 %collective-permute-start.119 = (bf16[2,512,512]{2,1,0:T(8,128)(2,1)S(1)}, bf16[2,512,512]{2,1,0:T(8,128)(2,1)S(1)}, u32[]{:S(2)}, u32[]{:S(2)}) collective-permute-start(bf16[2,512,512]{2,1,0:T(8,128)(2,1)S(1)} %copy-done.47), channel_id=1, source_target_pairs={{0,4},{4,0},{8,12},{12,8},{16,20},{20,16},{24,28},{28,24},{1,5},{5... | collective-permute-start | bytes 3145736 | tf_op jit(solution)/shard_map/ppermute | solution.py:36
  295.6 27.9 %collective-permute-start.92 = (bf16[512,128]{1,0:T(8,128)(2,1)S(1)}, bf16[512,128]{1,0:T(8,128)(2,1)S(1)}, u32[]{:S(2)}, u32[]{:S(2)}) collective-permute-start(bf16[512,128]{1,0:T(8,128)(2,1)S(1)} %get-tuple-element.254), channel_id=1, source_target_pairs={{0,4},{4,0},{8,12},{12,8},{16,20},{20,16},{24,28},{28,24},{1,5},{5... | collective-permute-start | bytes 393224 | tf_op jit(solution)/shard_map/ppermute | solution.py:36
  297.6 28.0 %collective-permute-start.104 = (bf16[512,128]{1,0:T(8,128)(2,1)S(1)}, bf16[512,128]{1,0:T(8,128)(2,1)S(1)}, u32[]{:S(2)}, u32[]{:S(2)}) collective-permute-start(bf16[512,128]{1,0:T(8,128)(2,1)S(1)} %get-tuple-element.252), channel_id=1, source_target_pairs={{0,4},{4,0},{8,12},{12,8},{16,20},{20,16},{24,28},{28,24},{1,5},{5... | collective-permute-start | bytes 393224 | tf_op jit(solution)/shard_map/ppermute | solution.py:36
  329.1 55.8 %collective-permute-start.91 = (bf16[2,512,512]{2,1,0:T(8,128)(2,1)}, bf16[2,512,512]{2,1,0:T(8,128)(2,1)}, u32[]{:S(2)}, u32[]{:S(2)}) collective-permute-start(bf16[2,512,512]{2,1,0:T(8,128)(2,1)} %get-tuple-element.155), channel_id=1, source_target_pairs={{0,4},{4,0},{8,12},{12,8},{16,20},{20,16},{24,28},{28,24},{1,5},{5... | collective-permute-start | bytes 3145736 | tf_op jit(solution)/shard_map/ppermute | solution.py:36
  373.7 26.0 %collective-permute-start.103 = (bf16[2,512,512]{2,1,0:T(8,128)(2,1)S(1)}, bf16[2,512,512]{2,1,0:T(8,128)(2,1)S(1)}, u32[]{:S(2)}, u32[]{:S(2)}) collective-permute-start(bf16[2,512,512]{2,1,0:T(8,128)(2,1)S(1)} %copy-done.50), channel_id=1, source_target_pairs={{0,4},{4,0},{8,12},{12,8},{16,20},{20,16},{24,28},{28,24},{1,5},{5... | collective-permute-start | bytes 3145736 | tf_op jit(solution)/shard_map/ppermute | solution.py:36
  374.6 51.3 %collective-permute-start.121 = (bf16[384,1152]{1,0:T(8,128)(2,1)}, bf16[384,1152]{1,0:T(8,128)(2,1)}, u32[]{:S(2)}, u32[]{:S(2)}) collective-permute-start(bf16[384,1152]{1,0:T(8,128)(2,1)} %get-tuple-element.130), channel_id=1, source_target_pairs={{0,8},{4,12},{1,9},{5,13},{2,10},{6,14},{3,11},{7,15}} | collective-permute-start | bytes 2654216 | tf_op jit(solution)/shard_map/ppermute | solution.py:288
  379.5 50.0 %collective-permute-start.47 = (bf16[128,1024]{0,1:T(8,128)(2,1)}, bf16[128,1024]{0,1:T(8,128)(2,1)}, u32[]{:S(2)}, u32[]{:S(2)}) collective-permute-start(bf16[128,1024]{0,1:T(8,128)(2,1)} %get-tuple-element.162), channel_id=1, source_target_pairs={{0,4},{4,0},{8,12},{12,8},{16,20},{20,16},{24,28},{28,24},{1,5},{5... | collective-permute-start | bytes 786440 | tf_op jit(solution)/shard_map/ppermute | solution.py:36
  380.7 39.4 %collective-permute-start.41 = (bf16[128,1024]{0,1:T(8,128)(2,1)}, bf16[128,1024]{0,1:T(8,128)(2,1)}, u32[]{:S(2)}, u32[]{:S(2)}) collective-permute-start(bf16[128,1024]{0,1:T(8,128)(2,1)} %get-tuple-element.159), channel_id=1, source_target_pairs={{0,4},{4,0},{8,12},{12,8},{16,20},{20,16},{24,28},{28,24},{1,5},{5... | collective-permute-start | bytes 786440 | tf_op jit(solution)/shard_map/ppermute | solution.py:36
  384.8 36.5 %collective-permute-start.43 = (bf16[128,1024]{0,1:T(8,128)(2,1)}, bf16[128,1024]{0,1:T(8,128)(2,1)}, u32[]{:S(2)}, u32[]{:S(2)}) collective-permute-start(bf16[128,1024]{0,1:T(8,128)(2,1)} %get-tuple-element.160), channel_id=1, source_target_pairs={{0,4},{4,0},{8,12},{12,8},{16,20},{20,16},{24,28},{28,24},{1,5},{5... | collective-permute-start | bytes 786440 | tf_op jit(solution)/shard_map/ppermute | solution.py:36
  420.1 34.1 %collective-permute-start.80 = (bf16[4,48,1536]{2,1,0:T(8,128)(2,1)S(1)}, bf16[4,48,1536]{2,1,0:T(8,128)(2,1)S(1)}, u32[]{:S(2)}, u32[]{:S(2)}) collective-permute-start(bf16[4,48,1536]{2,1,0:T(8,128)(2,1)S(1)} %copy-done.57), channel_id=1, source_target_pairs={{0,4},{4,0},{8,12},{12,8},{16,20},{20,16},{24,28},{28,24},{1,5},{5... | collective-permute-start | bytes 1769480 | tf_op jit(solution)/shard_map/ppermute | solution.py:36
  424.6 26.2 %collective-permute-start.44 = (bf16[128,1024]{0,1:T(8,128)(2,1)S(1)}, bf16[128,1024]{0,1:T(8,128)(2,1)S(1)}, u32[]{:S(2)}, u32[]{:S(2)}) collective-permute-start(bf16[128,1024]{0,1:T(8,128)(2,1)S(1)} %get-tuple-element.157), channel_id=1, source_target_pairs={{16,0},{20,4},{24,8},{28,12},{17,1},{21,5},{25,9},{29,13},{18,2},{... | collective-permute-start | bytes 786440 | tf_op jit(solution)/shard_map/ppermute | solution.py:102
  426.0 24.9 %collective-permute-start.42 = (bf16[128,1024]{0,1:T(8,128)(2,1)S(1)}, bf16[128,1024]{0,1:T(8,128)(2,1)S(1)}, u32[]{:S(2)}, u32[]{:S(2)}) collective-permute-start(bf16[128,1024]{0,1:T(8,128)(2,1)S(1)} %get-tuple-element.156), channel_id=1, source_target_pairs={{24,0},{28,4},{25,1},{29,5},{26,2},{30,6},{27,3},{31,7}} | collective-permute-start | bytes 786440 | tf_op jit(solution)/shard_map/ppermute | solution.py:102
  429.6 44.9 %collective-permute-start.52 = (bf16[128,384]{0,1:T(8,128)(2,1)S(1)}, bf16[128,384]{0,1:T(8,128)(2,1)S(1)}, u32[]{:S(2)}, u32[]{:S(2)}) collective-permute-start(bf16[128,384]{0,1:T(8,128)(2,1)S(1)} %bitcast.734), channel_id=1, source_target_pairs={{0,3},{1,2},{2,1},{3,0},{4,7},{5,6},{6,5},{7,4},{8,11},{9,10},{10,... | collective-permute-start | bytes 294920 | tf_op jit(solution)/shard_map/ppermute | solution.py:36
  433.3 41.7 %collective-permute-start.51 = (bf16[128,384]{0,1:T(8,128)(2,1)S(1)}, bf16[128,384]{0,1:T(8,128)(2,1)S(1)}, u32[]{:S(2)}, u32[]{:S(2)}) collective-permute-start(bf16[128,384]{0,1:T(8,128)(2,1)S(1)} %bitcast.733), channel_id=1, source_target_pairs={{0,2},{1,3},{2,0},{3,1},{4,6},{5,7},{6,4},{7,5},{8,10},{9,11},{10,... | collective-permute-start | bytes 294920 | tf_op jit(solution)/shard_map/ppermute | solution.py:36
  450.9 25.5 %collective-permute-start.50 = (bf16[128,384]{0,1:T(8,128)(2,1)S(1)}, bf16[128,384]{0,1:T(8,128)(2,1)S(1)}, u32[]{:S(2)}, u32[]{:S(2)}) collective-permute-start(bf16[128,384]{0,1:T(8,128)(2,1)S(1)} %bitcast.732), channel_id=1, source_target_pairs={{0,1},{1,0},{2,3},{3,2},{4,5},{5,4},{6,7},{7,6},{8,9},{9,8},{10,11... | collective-permute-start | bytes 294920 | tf_op jit(solution)/shard_map/ppermute | solution.py:36
  474.5 45.4 %collective-permute-start.62 = (bf16[128,1024]{0,1:T(8,128)(2,1)}, bf16[128,1024]{0,1:T(8,128)(2,1)}, u32[]{:S(2)}, u32[]{:S(2)}) collective-permute-start(bf16[128,1024]{0,1:T(8,128)(2,1)} %add_convert_fusion), channel_id=1, source_target_pairs={{0,1},{1,0},{2,3},{3,2},{4,5},{5,4},{6,7},{7,6},{8,9},{9,8},{10,11... | collective-permute-start | bytes 786440 | tf_op jit(solution)/shard_map/ppermute | solution.py:36
  478.6 42.7 %collective-permute-start.63 = (bf16[128,1024]{0,1:T(8,128)(2,1)}, bf16[128,1024]{0,1:T(8,128)(2,1)}, u32[]{:S(2)}, u32[]{:S(2)}) collective-permute-start(bf16[128,1024]{0,1:T(8,128)(2,1)} %collective-permute-done.48), channel_id=1, source_target_pairs={{0,1},{1,0},{2,3},{3,2},{4,5},{5,4},{6,7},{7,6},{8,9},{9,8},{10,11... | collective-permute-start | bytes 786440 | tf_op jit(solution)/shard_map/ppermute | solution.py:36
  507.0 69.7 %collective-permute-start.124 = (bf16[384,1152]{1,0:T(8,128)(2,1)}, bf16[384,1152]{1,0:T(8,128)(2,1)}, u32[]{:S(2)}, u32[]{:S(2)}) collective-permute-start(bf16[384,1152]{1,0:T(8,128)(2,1)} %get-tuple-element.131), channel_id=1, source_target_pairs={{28,20},{24,16},{29,21},{25,17},{30,22},{26,18},{31,23},{27,19}} | collective-permute-start | bytes 2654216 | tf_op jit(solution)/shard_map/ppermute | solution.py:289
  508.6 24.7 %collective-permute-start.93 = (bf16[384,1152]{1,0:T(8,128)(2,1)}, bf16[384,1152]{1,0:T(8,128)(2,1)}, u32[]{:S(2)}, u32[]{:S(2)}) collective-permute-start(bf16[384,1152]{1,0:T(8,128)(2,1)} %get-tuple-element.138), channel_id=1, source_target_pairs={{0,8},{4,12},{1,9},{5,13},{2,10},{6,14},{3,11},{7,15}} | collective-permute-start | bytes 2654216 | tf_op jit(solution)/shard_map/ppermute | solution.py:288
  513.9 141.1 %collective-permute-start.96 = (bf16[384,1152]{1,0:T(8,128)(2,1)}, bf16[384,1152]{1,0:T(8,128)(2,1)}, u32[]{:S(2)}, u32[]{:S(2)}) collective-permute-start(bf16[384,1152]{1,0:T(8,128)(2,1)} %get-tuple-element.139), channel_id=1, source_target_pairs={{28,20},{24,16},{29,21},{25,17},{30,22},{26,18},{31,23},{27,19}} | collective-permute-start | bytes 2654216 | tf_op jit(solution)/shard_map/ppermute | solution.py:289
  519.9 42.3 %collective-permute-start.105 = (bf16[384,1152]{1,0:T(8,128)(2,1)}, bf16[384,1152]{1,0:T(8,128)(2,1)S(1)}, u32[]{:S(2)}, u32[]{:S(2)}) collective-permute-start(bf16[384,1152]{1,0:T(8,128)(2,1)} %get-tuple-element.134), channel_id=1, source_target_pairs={{0,8},{4,12},{1,9},{5,13},{2,10},{6,14},{3,11},{7,15}} | collective-permute-start | bytes 2654216 | tf_op jit(solution)/shard_map/ppermute | solution.py:288
  524.4 53.4 %collective-permute-start.122 = (bf16[384,1152]{1,0:T(8,128)(2,1)S(1)}, bf16[384,1152]{1,0:T(8,128)(2,1)S(1)}, u32[]{:S(2)}, u32[]{:S(2)}) collective-permute-start(bf16[384,1152]{1,0:T(8,128)(2,1)S(1)} %copy-done.53), channel_id=1, source_target_pairs={{0,8},{4,12},{8,16},{12,20},{1,9},{5,13},{9,17},{13,21},{2,10},{6,... | collective-permute-start | bytes 2654216 | tf_op jit(solution)/shard_map/ppermute | solution.py:288
  533.3 40.1 %collective-permute-start.83 = (bf16[48,1536]{1,0:T(8,128)(2,1)S(1)}, bf16[48,1536]{1,0:T(8,128)(2,1)S(1)}, u32[]{:S(2)}, u32[]{:S(2)}) collective-permute-start(bf16[48,1536]{1,0:T(8,128)(2,1)S(1)} %copy-done.75), channel_id=1, source_target_pairs={{0,8},{4,12},{8,16},{12,20},{16,24},{20,28},{1,9},{5,13},{9,17},{1... | collective-permute-start | bytes 442376 | tf_op jit(solution)/shard_map/ppermute | solution.py:288
  573.4 107.3 %collective-permute-start.108 = (bf16[384,1152]{1,0:T(8,128)(2,1)}, bf16[384,1152]{1,0:T(8,128)(2,1)}, u32[]{:S(2)}, u32[]{:S(2)}) collective-permute-start(bf16[384,1152]{1,0:T(8,128)(2,1)} %get-tuple-element.135), channel_id=1, source_target_pairs={{28,20},{24,16},{29,21},{25,17},{30,22},{26,18},{31,23},{27,19}} | collective-permute-start | bytes 2654216 | tf_op jit(solution)/shard_map/ppermute | solution.py:289
  577.8 81.1 %collective-permute-start.94 = (bf16[384,1152]{1,0:T(8,128)(2,1)}, bf16[384,1152]{1,0:T(8,128)(2,1)}, u32[]{:S(2)}, u32[]{:S(2)}) collective-permute-start(bf16[384,1152]{1,0:T(8,128)(2,1)} %fusion.27), channel_id=1, source_target_pairs={{0,8},{4,12},{8,16},{12,20},{1,9},{5,13},{9,17},{13,21},{2,10},{6,... | collective-permute-start | bytes 2654216 | tf_op jit(solution)/shard_map/ppermute | solution.py:288
  647.8 34.5 %collective-permute-start.106 = (bf16[384,1152]{1,0:T(8,128)(2,1)}, bf16[384,1152]{1,0:T(8,128)(2,1)S(1)}, u32[]{:S(2)}, u32[]{:S(2)}) collective-permute-start(bf16[384,1152]{1,0:T(8,128)(2,1)} %fusion.22), channel_id=1, source_target_pairs={{0,8},{4,12},{8,16},{12,20},{1,9},{5,13},{9,17},{13,21},{2,10},{6,... | collective-permute-start | bytes 2654216 | tf_op jit(solution)/shard_map/ppermute | solution.py:288
  655.0 36.7 %collective-permute-start.123 = (bf16[384,1152]{1,0:T(8,128)(2,1)}, bf16[384,1152]{1,0:T(8,128)(2,1)S(1)}, u32[]{:S(2)}, u32[]{:S(2)}) collective-permute-start(bf16[384,1152]{1,0:T(8,128)(2,1)} %get-tuple-element.128), channel_id=1, source_target_pairs={{0,8},{4,12},{8,16},{12,20},{16,24},{20,28},{1,9},{5,13},{9,17},{1... | collective-permute-start | bytes 2654216 | tf_op jit(solution)/shard_map/ppermute | solution.py:288
  662.2 81.6 %collective-permute-start.95 = (bf16[384,1152]{1,0:T(8,128)(2,1)S(1)}, bf16[384,1152]{1,0:T(8,128)(2,1)S(1)}, u32[]{:S(2)}, u32[]{:S(2)}) collective-permute-start(bf16[384,1152]{1,0:T(8,128)(2,1)S(1)} %get-tuple-element.136), channel_id=1, source_target_pairs={{0,8},{4,12},{8,16},{12,20},{16,24},{20,28},{1,9},{5,13},{9,17},{1... | collective-permute-start | bytes 2654216 | tf_op jit(solution)/shard_map/ppermute | solution.py:288
  684.9 58.9 %collective-permute-start.98 = (bf16[384,1152]{1,0:T(8,128)(2,1)S(1)}, bf16[384,1152]{1,0:T(8,128)(2,1)S(1)}, u32[]{:S(2)}, u32[]{:S(2)}) collective-permute-start(bf16[384,1152]{1,0:T(8,128)(2,1)S(1)} %fusion.26), channel_id=1, source_target_pairs={{28,20},{24,16},{20,12},{16,8},{12,4},{8,0},{29,21},{25,17},{21,13... | collective-permute-start | bytes 2654216 | tf_op jit(solution)/shard_map/ppermute | solution.py:289
  712.5 29.2 %collective-permute-start.128 = (bf16[48,256]{1,0:T(8,128)(2,1)S(1)}, bf16[48,256]{1,0:T(8,128)(2,1)S(1)}, u32[]{:S(2)}, u32[]{:S(2)}) collective-permute-start(bf16[48,256]{1,0:T(8,128)(2,1)S(1)} %get-tuple-element.263), channel_id=1, source_target_pairs={{0,3},{1,2},{2,1},{3,0},{4,7},{5,6},{6,5},{7,4},{8,11},{9,10},{10,... | collective-permute-start | bytes 73736 | tf_op jit(solution)/shard_map/ppermute | solution.py:36
  712.5 30.5 %collective-permute-start.130 = (bf16[48,256]{1,0:T(8,128)(2,1)S(1)}, bf16[48,256]{1,0:T(8,128)(2,1)S(1)}, u32[]{:S(2)}, u32[]{:S(2)}) collective-permute-start(bf16[48,256]{1,0:T(8,128)(2,1)S(1)} %get-tuple-element.262), channel_id=1, source_target_pairs={{0,1},{1,0},{2,3},{3,2},{4,5},{5,4},{6,7},{7,6},{8,9},{9,8},{10,11... | collective-permute-start | bytes 73736 | tf_op jit(solution)/shard_map/ppermute | solution.py:36
  715.0 45.4 %collective-permute-start.107 = (bf16[384,1152]{1,0:T(8,128)(2,1)S(1)}, bf16[384,1152]{1,0:T(8,128)(2,1)S(1)}, u32[]{:S(2)}, u32[]{:S(2)}) collective-permute-start(bf16[384,1152]{1,0:T(8,128)(2,1)S(1)} %get-tuple-element.132), channel_id=1, source_target_pairs={{0,8},{4,12},{8,16},{12,20},{16,24},{20,28},{1,9},{5,13},{9,17},{1... | collective-permute-start | bytes 2654216 | tf_op jit(solution)/shard_map/ppermute | solution.py:288
  (257 other events, 2164.0 us)
